TPU v7x, 256 devices: a whole 4x4x8 slice. The times are simulated.
256 devices in a mesh: dir: 16 (over y_lo, x, core), box: 16 (over z, y_hi).
Axes of the slice: x: 4, y: 4 (y_hi: 2, y_lo: 2; y = y_hi * 2 + y_lo), z: 8, core: 2. Of those that a mesh axis runs over, the one named last changes fastest.
Arguments:
- child_patterns: float32 [2, 128, 8, 128, 256], P(None, 'box', None, 'dir'), may hold values from -6 to 6
- translation: float32 [32, 2, 256, 512], P(None, None, 'dir'), may hold values from -1.5 to 1.5
- source_list: int32 [128, 24], P('box'), may hold values from -1 to 127, as said below
- operator_list: int32 [128, 24], P('box'), may hold values from 0 to 31
Outputs:
- incoming: float32 [2, 128, 8, 128, 256], P(None, 'box', None, 'dir')
Inputs may be any that keep to these rules, and one draw needn't show every extreme that they name: `source_list`: each row names distinct boxes other than the row's own box, then -1 in every unused entry; at least one row is full.
All inputs are finite; a program needn't handle non-finite values.
Results may differ from a plain program's by a relative error of at most 0.0003.
Values sent between devices are 32-bit elements; how exact they have to be, the bound alone decides.
No kernel may reach another device: no remote copies, remote signals or barrier semaphores. Data moves between devices by JAX's collectives and lax.ppermute only.
A program may use at most 192 MiB of HBM per device.

v0:
```python
import jax
import jax.numpy as jnp
from jax import lax
from jax.sharding import PartitionSpec as P

theta_even = (-0.0390625, 0.2734375, 0.8203125, -0.0546875)
theta_odd = (-0.0546875, 0.8203125, 0.2734375, -0.0390625)
phi_edge = -0.0625
phi_middle = 0.5625


def extended_2(value, sides, width):
    for axis, dim in sides:
        size, length = (lax.axis_size(axis), value.shape[dim])
        up = [(i, (i + 1) % size) for i in range(size - 1)]
        down = [(j, i) for i, j in up]
        last = lax.slice_in_dim(value, length - width, length, axis=dim)
        initial = lax.slice_in_dim(value, 0, width, axis=dim)
        before = lax.ppermute(last, axis, up)
        after = lax.ppermute(initial, axis, down)
        value = jnp.concatenate([before, value, after], axis=dim)
    return value


def from_behind(value, axis, steps):
    count = lax.axis_size(axis)
    pairs = [(source, (source + steps) % count) for source in range(count)]
    return lax.ppermute(value, axis, pairs)


def azimuth_table(child_cols):
    source = jnp.arange(child_cols, dtype=jnp.int32)[:, None]
    target = jnp.arange(2 * child_cols, dtype=jnp.int32)[None, :]
    base = target // 2
    is_odd = target % 2 == 1
    offset = (source - base) % child_cols
    odd_coef = (
        jnp.where(offset == child_cols - 1, phi_edge, 0.0)
        + jnp.where(offset == 0, phi_middle, 0.0)
        + jnp.where(offset == 1, phi_middle, 0.0)
        + jnp.where(offset == 2 % child_cols, phi_edge, 0.0)
    )
    even_coef = jnp.where(offset == 0, 1.0, 0.0)
    return jnp.where(is_odd, odd_coef, even_coef).astype(jnp.float32)


def polar_table(row_count):
    target = jnp.arange(2 * row_count, dtype=jnp.int32)[:, None]
    source = jnp.arange(row_count + 4, dtype=jnp.int32)[None, :]
    is_odd = target % 2 == 1
    offset = source - target // 2 - target % 2
    table = jnp.zeros((2 * row_count, row_count + 4), jnp.float32)
    for index in range(4):
        coef = jnp.where(is_odd, theta_odd[index], theta_even[index])
        table = table + jnp.where(offset == index, coef, 0.0).astype(jnp.float32)
    return table


def back_table(row_count):
    target = jnp.arange(row_count, dtype=jnp.int32)[:, None]
    source = jnp.arange(2 * row_count + 6, dtype=jnp.int32)[None, :]
    is_odd = source % 2 == 1
    offset = 3 + target - source // 2
    table = jnp.zeros((row_count, 2 * row_count + 6), jnp.float32)
    for index in range(4):
        coef = jnp.where(is_odd, theta_even[index], theta_odd[index])
        table = table + jnp.where(offset == index, coef, 0.0).astype(jnp.float32)
    return table


def mix_rows(table, values):
    return jnp.einsum("jk,abckp->abcjp", table, values, precision=lax.Precision.HIGHEST)


def mix_cols(values, table):
    return jnp.einsum("abcrk,kp->abcrp", values, table, precision=lax.Precision.HIGHEST)


def mix_cols_back(values, table):
    return jnp.einsum("abcrp,kp->abcrk", values, table, precision=lax.Precision.HIGHEST)


def phases(row_index, total_rows, total_cols):
    polar = (row_index.astype(jnp.float32) + 0.5) * (jnp.pi / total_rows)
    azimuth = jnp.arange(total_cols, dtype=jnp.float32) * (2.0 * jnp.pi / total_cols)
    octant = jnp.arange(8, dtype=jnp.int32)
    sign_x = (octant % 2 * 2 - 1).astype(jnp.float32)[:, None, None]
    sign_y = (octant // 2 % 2 * 2 - 1).astype(jnp.float32)[:, None, None]
    sign_z = (octant // 4 * 2 - 1).astype(jnp.float32)[:, None, None]
    wave_size = 0.125 * total_rows
    sin_polar = jnp.sin(polar)[None, :, None]
    cos_polar = jnp.cos(polar)[None, :, None]
    angle_table = wave_size * (
        sign_x * sin_polar * jnp.cos(azimuth)[None, None, :]
        + sign_y * sin_polar * jnp.sin(azimuth)[None, None, :]
        + sign_z * cos_polar
    )
    return (jnp.cos(angle_table), jnp.sin(angle_table))


def add_range(total_field, patterns_in, first_box, source_list, operator_hits, translation):
    width = patterns_in.shape[1]
    slots = first_box + jnp.arange(width, dtype=jnp.int32)
    selector = (source_list[:, :, None] == slots[None, None, :]).astype(jnp.float32)
    counts = jnp.einsum("dks,dkn->dsn", selector, operator_hits, precision=lax.Precision.HIGHEST)
    weights = jnp.einsum("dsn,ncrp->dscrp", counts, translation, precision=lax.Precision.HIGHEST)
    real_part = jnp.sum(
        weights[:, :, 0] * patterns_in[0][None] - weights[:, :, 1] * patterns_in[1][None], axis=1
    )
    imag_part = jnp.sum(
        weights[:, :, 0] * patterns_in[1][None] + weights[:, :, 1] * patterns_in[0][None], axis=1
    )
    return total_field + jnp.stack([real_part, imag_part])


def on_device(child_patterns, translation, source_list, operator_list):
    half_rows = child_patterns.shape[3]
    local_rows = 2 * half_rows
    child_cols = child_patterns.shape[4]
    total_cols = 2 * child_cols
    total_rows = local_rows * lax.axis_size("dir")
    first_row = lax.axis_index("dir") * local_rows
    az_table = azimuth_table(child_cols)
    padded = extended_2(child_patterns, (("dir", 3),), 2)
    refined = mix_cols(mix_rows(polar_table(half_rows), padded), az_table)
    cosine, sine_part = phases(
        first_row + jnp.arange(local_rows, dtype=jnp.int32), total_rows, total_cols
    )
    real_part = refined[0] * cosine[None] + refined[1] * sine_part[None]
    imag_part = refined[1] * cosine[None] - refined[0] * sine_part[None]
    parent = jnp.stack([jnp.sum(real_part, axis=1), jnp.sum(imag_part, axis=1)])
    box_count = lax.axis_size("box")
    my_index = lax.axis_index("box")
    width = parent.shape[1]
    op_count = translation.shape[0]
    operator_hits = (
        operator_list[:, :, None] == jnp.arange(op_count, dtype=jnp.int32)[None, None, :]
    ).astype(jnp.float32)
    empty = jnp.zeros(parent.shape, jnp.float32)
    received = add_range(empty, parent, my_index * width, source_list, operator_hits, translation)

    def cycle_turn(step, carry):
        total_field, patterns_in = carry
        patterns_in = from_behind(patterns_in, "box", 1)
        owner_index = (my_index - step) % box_count
        return (
            add_range(
                total_field,
                patterns_in,
                owner_index * width,
                source_list,
                operator_hits,
                translation,
            ),
            patterns_in,
        )

    received, _ = lax.fori_loop(1, box_count, cycle_turn, (received, parent))
    real_part = received[0][:, None] * cosine[None] - received[1][:, None] * sine_part[None]
    imag_part = received[1][:, None] * cosine[None] + received[0][:, None] * sine_part[None]
    shifted = mix_cols_back(jnp.stack([real_part, imag_part]), az_table)
    extended = extended_2(shifted, (("dir", 3),), 3)
    return mix_rows(back_table(half_rows), extended)


def solution(mesh):
    return jax.shard_map(
        on_device,
        mesh=mesh,
        in_specs=(
            P(None, "box", None, "dir", None),
            P(None, None, "dir", None),
            P("box", None),
            P("box", None),
        ),
        out_specs=P(None, "box", None, "dir", None),
        check_vma=False,
    )
```

profile of v0, /device:TPU:1, one launch (start us, length us, event | category | flops | bytes accessed | tf_op | source)
XLA Modules:
  0.0 321.9 jit_solution(15006878655725143585)
XLA Ops:
  2.6 4.5 %collective-permute-start.1 = (f32[2,8,8,2,256]{4,2,3,1,0:T(8,128)}, f32[2,8,8,2,256]{4,2,3,1,0:T(8,128)}, u32[]{:S(2)}, u32[]{:S(2)}) collective-permute-start(f32[2,8,8,2,256]{4,2,3,1,0:T(8,128)} %copy.27), channel_id=1, source_target_pairs={{0,16},{16,32},{32,48},{48,64},{64,80},{80,96},{96,112},{112,128},... | collective-permute-start | bytes 786440 | tf_op jit(solution)/shard_map/ppermute | solution.py:19
  11.1 5.8 %fusion.27 = f32[8,8,2,16,512]{4,1,3,2,0:T(8,128)} fusion(f32[8,8,32,1,1]{2,1,4,3,0:T(8,128)S(1)} %convolution_bitcast_fusion.1, f32[32,2,16,512]{3,2,1,0:T(8,128)S(1)} %copy-done.1), kind=kOutput, calls=%fused_computation.40 | convolution fusion | flops 402653184 | bytes 6299648 | tf_op jit(solution)/shard_map/dsn,ncrp->dscrp/dot_general | solution.py:106
  24.1 3.9 %fusion.25 = f32[2,8,8,16,512]{4,3,2,1,0:T(8,128)S(1)} fusion(f32[2,8,8,256,16]{3,4,2,1,0:T(8,128)S(1)} %fusion.19, s32[512]{0:T(512)S(1)} %add_select_fusion.1, pred[512]{0:T(512)(128)(4,1)S(1)} %fusion.79), kind=kOutput, calls=%fused_computation.38 | convolution fusion | flops 3224502272 | bytes 6294016 | tf_op jit(solution)/shard_map/abcrk,kp->abcrp/dot_general | solution.py:76
  31.9 251.7 %while.18 = (s32[]{:T(128)}, f32[2,8,16,512]{3,2,1,0:T(8,128)S(1)}, f32[2,8,16,512]{3,1,2,0:T(8,128)}, s32[8,24]{1,0:T(8,128)S(1)}, s32[]{:T(128)}, /*index=5*/f...) while((s32[]{:T(128)}, f32[2,8,16,512]{3,2,1,0:T(8,128)S(1)}, ...), condition=%wide.region_7.8_spmd.clone, body=%wide.region_4.7_spmd.clone.sunk | while | flops 407582240 | bytes 17319780 | solution.py:158
  34.7 3.4 %fusion.156 = f32[8,8,2,16,512]{4,1,3,2,0:T(8,128)S(1)} fusion(f32[8,8,32,1,1]{2,1,4,3,0:T(8,128)S(1)} %convolution_bitcast_fusion.3, f32[32,2,16,512]{3,0,2,1:T(8,128)S(1)} %get-tuple-element.344), kind=kOutput, calls=%fused_computation.3.clone.1 | convolution fusion | flops 402653184 | bytes 6299648 | tf_op jit(solution)/shard_map/while/body/eval_jaxpr/dsn,ncrp->dscrp/dot_general | solution.py:106
  38.1 12.9 %collective-permute-done = f32[2,8,16,512]{3,1,2,0:T(8,128)S(1)} collective-permute-done((f32[2,8,16,512]{3,1,2,0:T(8,128)}, f32[2,8,16,512]{3,1,2,0:T(8,128)S(1)}, u32[]{:S(2)}, u32[]{:S(2)}) %collective-permute-start) | collective-permute-done | bytes 524320 | tf_op jit(solution)/shard_map/while/body/eval_jaxpr/ppermute | solution.py:28
  54.0 3.4 %fusion.156 = f32[8,8,2,16,512]{4,1,3,2,0:T(8,128)S(1)} fusion(f32[8,8,32,1,1]{2,1,4,3,0:T(8,128)S(1)} %convolution_bitcast_fusion.3, f32[32,2,16,512]{3,0,2,1:T(8,128)S(1)} %get-tuple-element.344), kind=kOutput, calls=%fused_computation.3.clone.1 | convolution fusion | flops 402653184 | bytes 6299648 | tf_op jit(solution)/shard_map/while/body/eval_jaxpr/dsn,ncrp->dscrp/dot_general | solution.py:106
  57.4 13.9 %collective-permute-done = f32[2,8,16,512]{3,1,2,0:T(8,128)S(1)} collective-permute-done((f32[2,8,16,512]{3,1,2,0:T(8,128)}, f32[2,8,16,512]{3,1,2,0:T(8,128)S(1)}, u32[]{:S(2)}, u32[]{:S(2)}) %collective-permute-start) | collective-permute-done | bytes 524320 | tf_op jit(solution)/shard_map/while/body/eval_jaxpr/ppermute | solution.py:28
  77.6 13.0 %collective-permute-done = f32[2,8,16,512]{3,1,2,0:T(8,128)S(1)} collective-permute-done((f32[2,8,16,512]{3,1,2,0:T(8,128)}, f32[2,8,16,512]{3,1,2,0:T(8,128)S(1)}, u32[]{:S(2)}, u32[]{:S(2)}) %collective-permute-start) | collective-permute-done | bytes 524320 | tf_op jit(solution)/shard_map/while/body/eval_jaxpr/ppermute | solution.py:28
  93.5 3.4 %fusion.156 = f32[8,8,2,16,512]{4,1,3,2,0:T(8,128)S(1)} fusion(f32[8,8,32,1,1]{2,1,4,3,0:T(8,128)S(1)} %convolution_bitcast_fusion.3, f32[32,2,16,512]{3,0,2,1:T(8,128)S(1)} %get-tuple-element.344), kind=kOutput, calls=%fused_computation.3.clone.1 | convolution fusion | flops 402653184 | bytes 6299648 | tf_op jit(solution)/shard_map/while/body/eval_jaxpr/dsn,ncrp->dscrp/dot_general | solution.py:106
  96.9 12.1 %collective-permute-done = f32[2,8,16,512]{3,1,2,0:T(8,128)S(1)} collective-permute-done((f32[2,8,16,512]{3,1,2,0:T(8,128)}, f32[2,8,16,512]{3,1,2,0:T(8,128)S(1)}, u32[]{:S(2)}, u32[]{:S(2)}) %collective-permute-start) | collective-permute-done | bytes 524320 | tf_op jit(solution)/shard_map/while/body/eval_jaxpr/ppermute | solution.py:28
  115.3 11.2 %collective-permute-done = f32[2,8,16,512]{3,1,2,0:T(8,128)S(1)} collective-permute-done((f32[2,8,16,512]{3,1,2,0:T(8,128)}, f32[2,8,16,512]{3,1,2,0:T(8,128)S(1)}, u32[]{:S(2)}, u32[]{:S(2)}) %collective-permute-start) | collective-permute-done | bytes 524320 | tf_op jit(solution)/shard_map/while/body/eval_jaxpr/ppermute | solution.py:28
  129.4 3.4 %fusion.156 = f32[8,8,2,16,512]{4,1,3,2,0:T(8,128)S(1)} fusion(f32[8,8,32,1,1]{2,1,4,3,0:T(8,128)S(1)} %convolution_bitcast_fusion.3, f32[32,2,16,512]{3,0,2,1:T(8,128)S(1)} %get-tuple-element.344), kind=kOutput, calls=%fused_computation.3.clone.1 | convolution fusion | flops 402653184 | bytes 6299648 | tf_op jit(solution)/shard_map/while/body/eval_jaxpr/dsn,ncrp->dscrp/dot_general | solution.py:106
  132.8 10.2 %collective-permute-done = f32[2,8,16,512]{3,1,2,0:T(8,128)S(1)} collective-permute-done((f32[2,8,16,512]{3,1,2,0:T(8,128)}, f32[2,8,16,512]{3,1,2,0:T(8,128)S(1)}, u32[]{:S(2)}, u32[]{:S(2)}) %collective-permute-start) | collective-permute-done | bytes 524320 | tf_op jit(solution)/shard_map/while/body/eval_jaxpr/ppermute | solution.py:28
  149.4 9.3 %collective-permute-done = f32[2,8,16,512]{3,1,2,0:T(8,128)S(1)} collective-permute-done((f32[2,8,16,512]{3,1,2,0:T(8,128)}, f32[2,8,16,512]{3,1,2,0:T(8,128)S(1)}, u32[]{:S(2)}, u32[]{:S(2)}) %collective-permute-start) | collective-permute-done | bytes 524320 | tf_op jit(solution)/shard_map/while/body/eval_jaxpr/ppermute | solution.py:28
  161.6 3.4 %fusion.156 = f32[8,8,2,16,512]{4,1,3,2,0:T(8,128)S(1)} fusion(f32[8,8,32,1,1]{2,1,4,3,0:T(8,128)S(1)} %convolution_bitcast_fusion.3, f32[32,2,16,512]{3,0,2,1:T(8,128)S(1)} %get-tuple-element.344), kind=kOutput, calls=%fused_computation.3.clone.1 | convolution fusion | flops 402653184 | bytes 6299648 | tf_op jit(solution)/shard_map/while/body/eval_jaxpr/dsn,ncrp->dscrp/dot_general | solution.py:106
  165.1 8.4 %collective-permute-done = f32[2,8,16,512]{3,1,2,0:T(8,128)S(1)} collective-permute-done((f32[2,8,16,512]{3,1,2,0:T(8,128)}, f32[2,8,16,512]{3,1,2,0:T(8,128)S(1)}, u32[]{:S(2)}, u32[]{:S(2)}) %collective-permute-start) | collective-permute-done | bytes 524320 | tf_op jit(solution)/shard_map/while/body/eval_jaxpr/ppermute | solution.py:28
  176.4 3.4 %fusion.156 = f32[8,8,2,16,512]{4,1,3,2,0:T(8,128)S(1)} fusion(f32[8,8,32,1,1]{2,1,4,3,0:T(8,128)S(1)} %convolution_bitcast_fusion.3, f32[32,2,16,512]{3,0,2,1:T(8,128)S(1)} %get-tuple-element.344), kind=kOutput, calls=%fused_computation.3.clone.1 | convolution fusion | flops 402653184 | bytes 6299648 | tf_op jit(solution)/shard_map/while/body/eval_jaxpr/dsn,ncrp->dscrp/dot_general | solution.py:106
  179.8 8.1 %collective-permute-done = f32[2,8,16,512]{3,1,2,0:T(8,128)S(1)} collective-permute-done((f32[2,8,16,512]{3,1,2,0:T(8,128)}, f32[2,8,16,512]{3,1,2,0:T(8,128)S(1)}, u32[]{:S(2)}, u32[]{:S(2)}) %collective-permute-start) | collective-permute-done | bytes 524320 | tf_op jit(solution)/shard_map/while/body/eval_jaxpr/ppermute | solution.py:28
  194.2 8.1 %collective-permute-done = f32[2,8,16,512]{3,1,2,0:T(8,128)S(1)} collective-permute-done((f32[2,8,16,512]{3,1,2,0:T(8,128)}, f32[2,8,16,512]{3,1,2,0:T(8,128)S(1)}, u32[]{:S(2)}, u32[]{:S(2)}) %collective-permute-start) | collective-permute-done | bytes 524320 | tf_op jit(solution)/shard_map/while/body/eval_jaxpr/ppermute | solution.py:28
  205.2 3.4 %fusion.156 = f32[8,8,2,16,512]{4,1,3,2,0:T(8,128)S(1)} fusion(f32[8,8,32,1,1]{2,1,4,3,0:T(8,128)S(1)} %convolution_bitcast_fusion.3, f32[32,2,16,512]{3,0,2,1:T(8,128)S(1)} %get-tuple-element.344), kind=kOutput, calls=%fused_computation.3.clone.1 | convolution fusion | flops 402653184 | bytes 6299648 | tf_op jit(solution)/shard_map/while/body/eval_jaxpr/dsn,ncrp->dscrp/dot_general | solution.py:106
  208.6 8.1 %collective-permute-done = f32[2,8,16,512]{3,1,2,0:T(8,128)S(1)} collective-permute-done((f32[2,8,16,512]{3,1,2,0:T(8,128)}, f32[2,8,16,512]{3,1,2,0:T(8,128)S(1)}, u32[]{:S(2)}, u32[]{:S(2)}) %collective-permute-start) | collective-permute-done | bytes 524320 | tf_op jit(solution)/shard_map/while/body/eval_jaxpr/ppermute | solution.py:28
  223.0 8.1 %collective-permute-done = f32[2,8,16,512]{3,1,2,0:T(8,128)S(1)} collective-permute-done((f32[2,8,16,512]{3,1,2,0:T(8,128)}, f32[2,8,16,512]{3,1,2,0:T(8,128)S(1)}, u32[]{:S(2)}, u32[]{:S(2)}) %collective-permute-start) | collective-permute-done | bytes 524320 | tf_op jit(solution)/shard_map/while/body/eval_jaxpr/ppermute | solution.py:28
  234.0 3.4 %fusion.156 = f32[8,8,2,16,512]{4,1,3,2,0:T(8,128)S(1)} fusion(f32[8,8,32,1,1]{2,1,4,3,0:T(8,128)S(1)} %convolution_bitcast_fusion.3, f32[32,2,16,512]{3,0,2,1:T(8,128)S(1)} %get-tuple-element.344), kind=kOutput, calls=%fused_computation.3.clone.1 | convolution fusion | flops 402653184 | bytes 6299648 | tf_op jit(solution)/shard_map/while/body/eval_jaxpr/dsn,ncrp->dscrp/dot_general | solution.py:106
  237.5 9.2 %collective-permute-done = f32[2,8,16,512]{3,1,2,0:T(8,128)S(1)} collective-permute-done((f32[2,8,16,512]{3,1,2,0:T(8,128)}, f32[2,8,16,512]{3,1,2,0:T(8,128)S(1)}, u32[]{:S(2)}, u32[]{:S(2)}) %collective-permute-start) | collective-permute-done | bytes 524320 | tf_op jit(solution)/shard_map/while/body/eval_jaxpr/ppermute | solution.py:28
  253.0 10.3 %collective-permute-done = f32[2,8,16,512]{3,1,2,0:T(8,128)S(1)} collective-permute-done((f32[2,8,16,512]{3,1,2,0:T(8,128)}, f32[2,8,16,512]{3,1,2,0:T(8,128)S(1)}, u32[]{:S(2)}, u32[]{:S(2)}) %collective-permute-start) | collective-permute-done | bytes 524320 | tf_op jit(solution)/shard_map/while/body/eval_jaxpr/ppermute | solution.py:28
  269.6 11.4 %collective-permute-done = f32[2,8,16,512]{3,1,2,0:T(8,128)S(1)} collective-permute-done((f32[2,8,16,512]{3,1,2,0:T(8,128)}, f32[2,8,16,512]{3,1,2,0:T(8,128)S(1)}, u32[]{:S(2)}, u32[]{:S(2)}) %collective-permute-start) | collective-permute-done | bytes 524320 | tf_op jit(solution)/shard_map/while/body/eval_jaxpr/ppermute | solution.py:28
  285.1 3.8 %fusion.9 = f32[2,8,8,16,256]{4,3,2,1,0:T(8,128)S(1)} fusion(f32[1,8,8,16,512]{4,3,2,1,0:T(8,128)S(1)} %get-tuple-element.239, f32[1,8,8,16,512]{4,3,2,1,0:T(8,128)S(1)} %get-tuple-element.238, s32[512]{0:T(512)S(1)} %add_select_fusion.1, pred[512]{0:T(512)(128)(4,1)S(1)} %fusion.79), kind=kOutput, calls=%fused_computation.18 | convolution fusion | flops 3225550848 | bytes 6294016 | tf_op jit(solution)/shard_map/abcrp,kp->abcrk/dot_general | solution.py:80
  289.2 18.6 %collective-permute-start.3 = (f32[2,8,8,3,256]{4,3,2,1,0:T(4,128)S(1)}, f32[2,8,8,3,256]{4,3,2,1,0:T(4,128)S(1)}, u32[]{:S(2)}, u32[]{:S(2)}) collective-permute-start(f32[2,8,8,3,256]{4,3,2,1,0:T(4,128)S(1)} %get-tuple-element.236), channel_id=1, source_target_pairs={{0,16},{16,32},{32,48},{48,64},{64,80},{80,96},{96,112},{112,128},... | collective-permute-start | bytes 1179656 | tf_op jit(solution)/shard_map/ppermute | solution.py:19
  310.0 3.9 %collective-permute-done.3 = f32[2,8,8,3,256]{4,3,2,1,0:T(4,128)S(1)} collective-permute-done((f32[2,8,8,3,256]{4,3,2,1,0:T(4,128)S(1)}, f32[2,8,8,3,256]{4,3,2,1,0:T(4,128)S(1)}, u32[]{:S(2)}, u32[]{:S(2)}) %collective-permute-start.3) | collective-permute-done | bytes 393248 | tf_op jit(solution)/shard_map/ppermute | solution.py:19
  313.8 4.4 %collective-permute-done.4 = f32[2,8,8,3,256]{4,3,2,1,0:T(4,128)S(1)} collective-permute-done((f32[2,8,8,3,256]{4,3,2,1,0:T(4,128)S(1)}, f32[2,8,8,3,256]{4,3,2,1,0:T(4,128)S(1)}, u32[]{:S(2)}, u32[]{:S(2)}) %collective-permute-start.4) | collective-permute-done | bytes 393248 | tf_op jit(solution)/shard_map/ppermute | solution.py:20
  318.2 3.6 %fusion.29 = f32[2,8,8,8,256]{4,3,2,1,0:T(8,128)} fusion(f32[2,8,8,3,256]{4,3,2,1,0:T(4,128)S(1)} %collective-permute-done.4, f32[2,8,8,16,256]{4,3,2,1,0:T(8,128)S(1)} %fusion.9, f32[2,8,8,3,256]{4,3,2,1,0:T(4,128)S(1)} %collective-permute-done.3, f32[22]{0:T(128)S(1)} %get-tuple-element.262, f32[22]{0:T(128)S(1)} %get-tuple-element.260, ...), kind=kOutput, calls=%fused_computation.48 | convolution fusion | flops 70649920 | bytes 3932632 | tf_op jit(solution)/shard_map/jk,abckp->abcjp/dot_general | solution.py:72
  (165 shorter events, 90.8 us)
Async XLA Ops:
  0.0 10.8 %copy-start.6 = (s32[8,24]{1,0:T(8,128)S(1)}, s32[8,24]{1,0:T(8,128)}, u32[]{:S(2)}) copy-start(s32[8,24]{1,0:T(8,128)} %param.8) | copy-start | bytes 2308
  0.0 10.8 %copy-start.5 = (s32[8,24]{1,0:T(8,128)S(1)}, s32[8,24]{1,0:T(8,128)}, u32[]{:S(2)}) copy-start(s32[8,24]{1,0:T(8,128)} %param.9) | copy-start | bytes 2308
  0.0 11.0 %copy-start.1 = (f32[32,2,16,512]{3,2,1,0:T(8,128)S(1)}, f32[32,2,16,512]{3,2,1,0:T(8,128)}, u32[]{:S(2)}) copy-start(f32[32,2,16,512]{3,2,1,0:T(8,128)} %param.7) | copy-start | bytes 6291460
  2.6 16.7 %collective-permute-start.1 = (f32[2,8,8,2,256]{4,2,3,1,0:T(8,128)}, f32[2,8,8,2,256]{4,2,3,1,0:T(8,128)}, u32[]{:S(2)}, u32[]{:S(2)}) collective-permute-start(f32[2,8,8,2,256]{4,2,3,1,0:T(8,128)} %copy.27), channel_id=1, source_target_pairs={{0,16},{16,32},{32,48},{48,64},{64,80},{80,96},{96,112},{112,128},... | collective-permute-start | bytes 786440 | tf_op jit(solution)/shard_map/ppermute | solution.py:19
  7.9 12.6 %collective-permute-start.2 = (f32[2,8,8,2,256]{4,2,3,1,0:T(8,128)}, f32[2,8,8,2,256]{4,2,3,1,0:T(8,128)}, u32[]{:S(2)}, u32[]{:S(2)}) collective-permute-start(f32[2,8,8,2,256]{4,2,3,1,0:T(8,128)} %copy.28), channel_id=1, source_target_pairs={{16,0},{32,16},{48,32},{64,48},{80,64},{96,80},{112,96},{128,112},... | collective-permute-start | bytes 786440 | tf_op jit(solution)/shard_map/ppermute | solution.py:20
  11.1 5.9 %copy-start.2 = (f32[32,2,16,512]{3,2,1,0:T(8,128)S(1)}, f32[32,2,16,512]{3,2,1,0:T(8,128)}, u32[]{:S(2)}) copy-start(f32[32,2,16,512]{3,2,1,0:T(8,128)} %param.7) | copy-start | bytes 6291460
  17.0 4.6 %copy-start.4 = (f32[2,8,8,8,256]{4,3,2,1,0:T(8,128)S(1)}, f32[2,8,8,8,256]{4,3,2,1,0:T(8,128)}, u32[]{:S(2)}) copy-start(f32[2,8,8,8,256]{4,3,2,1,0:T(8,128)} %param.6) | copy-start | bytes 3145732
  19.3 8.7 %copy-start.3 = (f32[8,16,512]{2,1,0:T(8,128)}, f32[8,16,512]{2,1,0:T(8,128)S(1)}, u32[]{:S(2)}) copy-start(f32[8,16,512]{2,1,0:T(8,128)S(1)} %get-tuple-element.245) | copy-start | bytes 786436
  28.0 2.2 copy-start
  32.1 19.0 %collective-permute-start = (f32[2,8,16,512]{3,1,2,0:T(8,128)}, f32[2,8,16,512]{3,1,2,0:T(8,128)S(1)}, u32[]{:S(2)}, u32[]{:S(2)}) collective-permute-start(f32[2,8,16,512]{3,1,2,0:T(8,128)} %get-tuple-element.329), channel_id=1, source_target_pairs={{0,1},{1,2},{2,3},{3,4},{4,5},{5,6},{6,7},{7,8},{8,9},{9,10},{10,1... | collective-permute-start | bytes 1572872 | tf_op jit(solution)/shard_map/while/body/eval_jaxpr/ppermute | solution.py:28
  53.6 17.6 %collective-permute-start = (f32[2,8,16,512]{3,1,2,0:T(8,128)}, f32[2,8,16,512]{3,1,2,0:T(8,128)S(1)}, u32[]{:S(2)}, u32[]{:S(2)}) collective-permute-start(f32[2,8,16,512]{3,1,2,0:T(8,128)} %get-tuple-element.329), channel_id=1, source_target_pairs={{0,1},{1,2},{2,3},{3,4},{4,5},{5,6},{6,7},{7,8},{8,9},{9,10},{10,1... | collective-permute-start | bytes 1572872 | tf_op jit(solution)/shard_map/while/body/eval_jaxpr/ppermute | solution.py:28
  73.8 16.8 %collective-permute-start = (f32[2,8,16,512]{3,1,2,0:T(8,128)}, f32[2,8,16,512]{3,1,2,0:T(8,128)S(1)}, u32[]{:S(2)}, u32[]{:S(2)}) collective-permute-start(f32[2,8,16,512]{3,1,2,0:T(8,128)} %get-tuple-element.329), channel_id=1, source_target_pairs={{0,1},{1,2},{2,3},{3,4},{4,5},{5,6},{6,7},{7,8},{8,9},{9,10},{10,1... | collective-permute-start | bytes 1572872 | tf_op jit(solution)/shard_map/while/body/eval_jaxpr/ppermute | solution.py:28
  93.2 15.8 %collective-permute-start = (f32[2,8,16,512]{3,1,2,0:T(8,128)}, f32[2,8,16,512]{3,1,2,0:T(8,128)S(1)}, u32[]{:S(2)}, u32[]{:S(2)}) collective-permute-start(f32[2,8,16,512]{3,1,2,0:T(8,128)} %get-tuple-element.329), channel_id=1, source_target_pairs={{0,1},{1,2},{2,3},{3,4},{4,5},{5,6},{6,7},{7,8},{8,9},{9,10},{10,1... | collective-permute-start | bytes 1572872 | tf_op jit(solution)/shard_map/while/body/eval_jaxpr/ppermute | solution.py:28
  111.6 14.9 %collective-permute-start = (f32[2,8,16,512]{3,1,2,0:T(8,128)}, f32[2,8,16,512]{3,1,2,0:T(8,128)S(1)}, u32[]{:S(2)}, u32[]{:S(2)}) collective-permute-start(f32[2,8,16,512]{3,1,2,0:T(8,128)} %get-tuple-element.329), channel_id=1, source_target_pairs={{0,1},{1,2},{2,3},{3,4},{4,5},{5,6},{6,7},{7,8},{8,9},{9,10},{10,1... | collective-permute-start | bytes 1572872 | tf_op jit(solution)/shard_map/while/body/eval_jaxpr/ppermute | solution.py:28
  129.1 14.0 %collective-permute-start = (f32[2,8,16,512]{3,1,2,0:T(8,128)}, f32[2,8,16,512]{3,1,2,0:T(8,128)S(1)}, u32[]{:S(2)}, u32[]{:S(2)}) collective-permute-start(f32[2,8,16,512]{3,1,2,0:T(8,128)} %get-tuple-element.329), channel_id=1, source_target_pairs={{0,1},{1,2},{2,3},{3,4},{4,5},{5,6},{6,7},{7,8},{8,9},{9,10},{10,1... | collective-permute-start | bytes 1572872 | tf_op jit(solution)/shard_map/while/body/eval_jaxpr/ppermute | solution.py:28
  145.6 13.1 %collective-permute-start = (f32[2,8,16,512]{3,1,2,0:T(8,128)}, f32[2,8,16,512]{3,1,2,0:T(8,128)S(1)}, u32[]{:S(2)}, u32[]{:S(2)}) collective-permute-start(f32[2,8,16,512]{3,1,2,0:T(8,128)} %get-tuple-element.329), channel_id=1, source_target_pairs={{0,1},{1,2},{2,3},{3,4},{4,5},{5,6},{6,7},{7,8},{8,9},{9,10},{10,1... | collective-permute-start | bytes 1572872 | tf_op jit(solution)/shard_map/while/body/eval_jaxpr/ppermute | solution.py:28
  161.3 12.2 %collective-permute-start = (f32[2,8,16,512]{3,1,2,0:T(8,128)}, f32[2,8,16,512]{3,1,2,0:T(8,128)S(1)}, u32[]{:S(2)}, u32[]{:S(2)}) collective-permute-start(f32[2,8,16,512]{3,1,2,0:T(8,128)} %get-tuple-element.329), channel_id=1, source_target_pairs={{0,1},{1,2},{2,3},{3,4},{4,5},{5,6},{6,7},{7,8},{8,9},{9,10},{10,1... | collective-permute-start | bytes 1572872 | tf_op jit(solution)/shard_map/while/body/eval_jaxpr/ppermute | solution.py:28
  176.0 11.9 %collective-permute-start = (f32[2,8,16,512]{3,1,2,0:T(8,128)}, f32[2,8,16,512]{3,1,2,0:T(8,128)S(1)}, u32[]{:S(2)}, u32[]{:S(2)}) collective-permute-start(f32[2,8,16,512]{3,1,2,0:T(8,128)} %get-tuple-element.329), channel_id=1, source_target_pairs={{0,1},{1,2},{2,3},{3,4},{4,5},{5,6},{6,7},{7,8},{8,9},{9,10},{10,1... | collective-permute-start | bytes 1572872 | tf_op jit(solution)/shard_map/while/body/eval_jaxpr/ppermute | solution.py:28
  190.4 11.9 %collective-permute-start = (f32[2,8,16,512]{3,1,2,0:T(8,128)}, f32[2,8,16,512]{3,1,2,0:T(8,128)S(1)}, u32[]{:S(2)}, u32[]{:S(2)}) collective-permute-start(f32[2,8,16,512]{3,1,2,0:T(8,128)} %get-tuple-element.329), channel_id=1, source_target_pairs={{0,1},{1,2},{2,3},{3,4},{4,5},{5,6},{6,7},{7,8},{8,9},{9,10},{10,1... | collective-permute-start | bytes 1572872 | tf_op jit(solution)/shard_map/while/body/eval_jaxpr/ppermute | solution.py:28
  204.9 11.9 %collective-permute-start = (f32[2,8,16,512]{3,1,2,0:T(8,128)}, f32[2,8,16,512]{3,1,2,0:T(8,128)S(1)}, u32[]{:S(2)}, u32[]{:S(2)}) collective-permute-start(f32[2,8,16,512]{3,1,2,0:T(8,128)} %get-tuple-element.329), channel_id=1, source_target_pairs={{0,1},{1,2},{2,3},{3,4},{4,5},{5,6},{6,7},{7,8},{8,9},{9,10},{10,1... | collective-permute-start | bytes 1572872 | tf_op jit(solution)/shard_map/while/body/eval_jaxpr/ppermute | solution.py:28
  219.3 11.9 %collective-permute-start = (f32[2,8,16,512]{3,1,2,0:T(8,128)}, f32[2,8,16,512]{3,1,2,0:T(8,128)S(1)}, u32[]{:S(2)}, u32[]{:S(2)}) collective-permute-start(f32[2,8,16,512]{3,1,2,0:T(8,128)} %get-tuple-element.329), channel_id=1, source_target_pairs={{0,1},{1,2},{2,3},{3,4},{4,5},{5,6},{6,7},{7,8},{8,9},{9,10},{10,1... | collective-permute-start | bytes 1572872 | tf_op jit(solution)/shard_map/while/body/eval_jaxpr/ppermute | solution.py:28
  233.7 13.0 %collective-permute-start = (f32[2,8,16,512]{3,1,2,0:T(8,128)}, f32[2,8,16,512]{3,1,2,0:T(8,128)S(1)}, u32[]{:S(2)}, u32[]{:S(2)}) collective-permute-start(f32[2,8,16,512]{3,1,2,0:T(8,128)} %get-tuple-element.329), channel_id=1, source_target_pairs={{0,1},{1,2},{2,3},{3,4},{4,5},{5,6},{6,7},{7,8},{8,9},{9,10},{10,1... | collective-permute-start | bytes 1572872 | tf_op jit(solution)/shard_map/while/body/eval_jaxpr/ppermute | solution.py:28
  249.2 14.0 %collective-permute-start = (f32[2,8,16,512]{3,1,2,0:T(8,128)}, f32[2,8,16,512]{3,1,2,0:T(8,128)S(1)}, u32[]{:S(2)}, u32[]{:S(2)}) collective-permute-start(f32[2,8,16,512]{3,1,2,0:T(8,128)} %get-tuple-element.329), channel_id=1, source_target_pairs={{0,1},{1,2},{2,3},{3,4},{4,5},{5,6},{6,7},{7,8},{8,9},{9,10},{10,1... | collective-permute-start | bytes 1572872 | tf_op jit(solution)/shard_map/while/body/eval_jaxpr/ppermute | solution.py:28
  265.8 15.1 %collective-permute-start = (f32[2,8,16,512]{3,1,2,0:T(8,128)}, f32[2,8,16,512]{3,1,2,0:T(8,128)S(1)}, u32[]{:S(2)}, u32[]{:S(2)}) collective-permute-start(f32[2,8,16,512]{3,1,2,0:T(8,128)} %get-tuple-element.329), channel_id=1, source_target_pairs={{0,1},{1,2},{2,3},{3,4},{4,5},{5,6},{6,7},{7,8},{8,9},{9,10},{10,1... | collective-permute-start | bytes 1572872 | tf_op jit(solution)/shard_map/while/body/eval_jaxpr/ppermute | solution.py:28
  289.2 24.7 %collective-permute-start.3 = (f32[2,8,8,3,256]{4,3,2,1,0:T(4,128)S(1)}, f32[2,8,8,3,256]{4,3,2,1,0:T(4,128)S(1)}, u32[]{:S(2)}, u32[]{:S(2)}) collective-permute-start(f32[2,8,8,3,256]{4,3,2,1,0:T(4,128)S(1)} %get-tuple-element.236), channel_id=1, source_target_pairs={{0,16},{16,32},{32,48},{48,64},{64,80},{80,96},{96,112},{112,128},... | collective-permute-start | bytes 1179656 | tf_op jit(solution)/shard_map/ppermute | solution.py:19
  307.7 10.5 %collective-permute-start.4 = (f32[2,8,8,3,256]{4,3,2,1,0:T(4,128)S(1)}, f32[2,8,8,3,256]{4,3,2,1,0:T(4,128)S(1)}, u32[]{:S(2)}, u32[]{:S(2)}) collective-permute-start(f32[2,8,8,3,256]{4,3,2,1,0:T(4,128)S(1)} %get-tuple-element.237), channel_id=1, source_target_pairs={{16,0},{32,16},{48,32},{64,48},{80,64},{96,80},{112,96},{128,112},... | collective-permute-start | bytes 1179656 | tf_op jit(solution)/shard_map/ppermute | solution.py:20
where the time goes:
time: 325 us; the launch traced here: 322 us
  waiting for transfers between devices  162 us (50%)
  matrix products  76.1 us (23%)
  other arithmetic  30.9 us (10%)
  starting transfers between devices  30.2 us (9%)
  local copies, waits for them, and re-layouts  21.1 us (6%)
    ppermute x15, waiting for transfers between devices, from_behind(): return lax.ppermute(value, axis, pairs)  154 us
    dot_general x16, matrix products, add_range(): jnp.einsum('dsn,ncrp->dscrp', counts, translation, precision=lax.Precisio...  57.1 us
    reduce_sum x16, other arithmetic, add_range(): jnp.sum(weights[:, :, 0] * patterns_in[0][None] - weights[:, :, 1] * patt...  25.2 us
    ppermute x2, starting transfers between devices, extended_2(): before = lax.ppermute(last, axis, up)  23.1 us
    while x15, local copies, waits for them, and re-layouts  11.9 us
  transfers between devices with their start and end apart: 19, of which 17 were waited for; matrix products, arithmetic and copies ran while one was open for 21% of the time, Pallas kernels for 0%

commit v1 on v0

v1 whole, which is shorter than its diff:
```python
import functools

import jax
import jax.numpy as jnp
from jax import lax
from jax.experimental import pallas as pl
from jax.experimental.pallas import tpu as pltpu
from jax.sharding import PartitionSpec as P

TAP = {
    -3: -0.0390625,
    -2: -0.0546875,
    -1: 0.2734375,
    0: 0.8203125,
    1: 0.8203125,
    2: 0.2734375,
    3: -0.0546875,
    4: -0.0390625,
}
KIDS = 8
HALO = 3
LANES = 128
CHUNK = 8
VMEM = 24 * 1024 * 1024


def tile_iota():
    sub = lax.broadcasted_iota(jnp.int32, (8, LANES), 0)
    lane = lax.broadcasted_iota(jnp.int32, (8, LANES), 1)
    return sub, lane


def swap_parts(tile):
    return jnp.concatenate([tile[4:8], tile[0:4]], axis=0)


def fill_phases(table, rows, first_row, total_rows, total_cols):
    sub, lane = tile_iota()
    block = sub % 4
    sample = 2 * ((block % 2) * LANES + lane) + block // 2
    azimuth = sample.astype(jnp.float32) * (2.0 * jnp.pi / total_cols)
    low = sub < 4
    course = jnp.where(low, jnp.cos(azimuth), jnp.sin(azimuth))
    wave = 0.125 * total_rows
    padded = -(-len(rows) // 8) * 8
    offset = lax.broadcasted_iota(jnp.int32, (padded, LANES), 0)
    number = jnp.zeros((padded, LANES), jnp.int32)
    for i, r in enumerate(rows):
        number = jnp.where(offset == i, r, number)
    polar = ((number + first_row).astype(jnp.float32) + 0.5) * (jnp.pi / total_rows)
    sin_polar = wave * jnp.sin(polar)
    height = wave * jnp.cos(polar)
    cos_z = jnp.cos(height)
    sin_z = jnp.sin(height)
    for i in range(len(rows)):
        angle = sin_polar[i : i + 1] * course
        cos_a, sin_a = jnp.cos(angle), jnp.sin(angle)
        cos_b, sin_b = swap_parts(cos_a), swap_parts(sin_a)
        cx, cy = jnp.where(low, cos_a, cos_b), jnp.where(low, cos_b, cos_a)
        sx, sy = jnp.where(low, sin_a, sin_b), jnp.where(low, sin_b, sin_a)
        cc, ss, sc, cs = cx * cy, sx * sy, sx * cy, cx * sy
        plus_c, plus_s = cc - ss, sc + cs
        minus_c, minus_s = cc + ss, sc - cs
        cz, sz = cos_z[i : i + 1], sin_z[i : i + 1]
        for p in range(4):
            x_up, y_up = p % 2 == 1, p // 2 == 1
            base_c, base_s = (plus_c, plus_s) if x_up == y_up else (minus_c, minus_s)
            if not x_up:
                base_s = -base_s
            at = (i * 4 + p) * 16
            table[at : at + 8, :] = base_c * cz - base_s * sz
            table[at + 8 : at + 16, :] = base_s * cz + base_c * sz


def azimuth_weights(cols, transpose):
    i = lax.broadcasted_iota(jnp.int32, (cols, cols), 0)
    j = lax.broadcasted_iota(jnp.int32, (cols, cols), 1)
    shift = (j - i if transpose else i - j) % cols
    near = (shift == 0) | (shift == 1)
    far = (shift == cols - 1) | (shift == 2)
    return jnp.where(near, 0.5625, jnp.where(far, -0.0625, 0.0)).astype(jnp.bfloat16)


def split_dot(values, weights):
    high = values.astype(jnp.bfloat16)
    rest = (values - high.astype(jnp.float32)).astype(jnp.bfloat16)
    both = jnp.concatenate([high, rest], axis=0)
    out = jnp.dot(both, weights, preferred_element_type=jnp.float32)
    count = values.shape[0]
    return out[:count] + out[count:]


def weighted(terms):
    total = None
    for coef, tile in terms:
        part = coef * tile
        total = part if total is None else total + part
    return total


def aggregate(x_ref, tiles, table, rows, first_row, total_rows, total_cols, store):
    boxes = x_ref.shape[1] // 64
    cols = x_ref.shape[2]
    fill_phases(table, rows, first_row, total_rows, total_cols)
    weights = azimuth_weights(cols, False)
    sub, _ = tile_iota()
    sign = jnp.where(sub < 4, 1.0, -1.0).astype(jnp.float32)

    def refine(b, carry):
        parts = []
        for part in range(2):
            kids = [x_ref[part, pl.ds(pl.multiple_of(b * 64 + c * 8, 8), 8), :] for c in range(KIDS)]
            both = [kids[4 + p] + kids[3 - p] for p in range(4)]
            both += [kids[4 + p] - kids[3 - p] for p in range(4)]
            parts.append(jnp.concatenate(both, axis=0))
        even = jnp.concatenate(parts, axis=0)
        odd = split_dot(even, weights)
        for part in range(2):
            for block in range(4):
                source = even if block < 2 else odd
                lanes = slice((block % 2) * LANES, (block % 2 + 1) * LANES)
                tiles[pl.ds(b * 512 + part * 4 + block, 64, stride=8), :] = source[
                    part * 64 : part * 64 + 64, lanes
                ]
        return carry

    lax.fori_loop(0, boxes, refine, 0)

    def combine(b, carry):
        for i, r in enumerate(rows):
            taps = [(TAP[r - 2 * k], k) for k in range(8) if r - 2 * k in TAP]
            total, turned = None, None
            for p in range(4):
                sums = []
                for q in (p, 4 + p):
                    sums.append(
                        weighted(
                            [
                                (
                                    coef,
                                    tiles[pl.ds(pl.multiple_of(b * 512 + (q * 8 + k) * 8, 8), 8), :],
                                )
                                for coef, k in taps
                            ]
                        )
                    )
                at = (i * 4 + p) * 16
                first = sums[0] * table[at : at + 8, :]
                second = sums[1] * table[at + 8 : at + 16, :]
                total = first if total is None else total + first
                turned = second if turned is None else turned + second
            store(i, b, total + swap_parts(turned) * sign)
        return carry

    lax.fori_loop(0, boxes, combine, 0)


def halo_kernel(total_rows, total_cols, x_ref, up_ref, down_ref, tiles, table):
    first_row = lax.axis_index("dir") * 16

    def store(i, b, tile):
        ref = up_ref if i < HALO else down_ref
        ref[pl.ds(pl.multiple_of((i % HALO) * 64 + b * 8, 8), 8), :] = tile

    rows = (-3, -2, -1, 16, 17, 18)
    aggregate(x_ref, tiles, table, rows, first_row, total_rows, total_cols, store)


def main_kernel(
    total_rows, total_cols, x_ref, note_ref, row_ref, out_ref, operator_ref, tiles, table
):
    first_row = lax.axis_index("dir") * 16

    def store(i, b, tile):
        out_ref[pl.ds(pl.multiple_of(i * 72 + b * 8, 8), 8), :] = tile

    aggregate(x_ref, tiles, table, tuple(range(16)), first_row, total_rows, total_cols, store)
    for r in range(16):
        out_ref[r * 72 + 64 : r * 72 + 72, :] = note_ref[...]
    count = row_ref.shape[0]
    wide = row_ref.shape[1]
    source = lax.broadcasted_iota(jnp.int32, (wide, wide), 0)
    target = lax.broadcasted_iota(jnp.int32, (wide, wide), 1)
    half = wide // 2
    wanted = jnp.where(target < half, 2 * target, 2 * (target - half) + 1)
    pick = jnp.where(source == wanted, 1.0, 0.0).astype(jnp.bfloat16)
    values = row_ref[...]
    high = values.astype(jnp.bfloat16)
    rest = values - high.astype(jnp.float32)
    middle = rest.astype(jnp.bfloat16)
    low = (rest - middle.astype(jnp.float32)).astype(jnp.bfloat16)
    three = jnp.dot(
        jnp.concatenate([high, middle, low], axis=0), pick, preferred_element_type=jnp.float32
    )
    sorted_row = three[:count] + three[count : 2 * count] + three[2 * count :]
    for block in range(4):
        part = sorted_row[:, block * LANES : (block + 1) * LANES]
        operator_ref[pl.ds(block, count, stride=8), :] = part
        operator_ref[pl.ds(block + 4, count, stride=8), :] = part
    operator_ref[count * 8 : count * 8 + 16, :] = jnp.zeros((16, LANES), jnp.float32)


def translate_kernel(x_ref, operator_ref, out_ref, notes, scalars, sem):
    groups = out_ref.shape[0] // 64
    for g in range(groups):
        notes[g * 4 : g * 4 + 4, :] = x_ref[g * 72 + 64 : g * 72 + 68, :].astype(jnp.int32)
    copy = pltpu.make_async_copy(notes, scalars, sem)
    copy.start()
    copy.wait()
    sub, _ = tile_iota()
    sign = jnp.where(sub < 4, -1.0, 1.0).astype(jnp.float32)
    zero = jnp.zeros((8, LANES), jnp.float32)

    def group(g, carry):
        for b in range(8):

            def step(c, sums):
                total, turned = sums
                entry = b * 24 + c * CHUNK
                row, lane = g * 4 + entry // LANES, entry % LANES
                firsts, seconds = [], []
                for k in range(CHUNK):
                    at = pl.multiple_of(scalars[row, lane + k], 8)
                    by = pl.multiple_of(scalars[row + 2, lane + k], 8)
                    pattern = x_ref[pl.ds(at, 8), :]
                    firsts.append(pattern * operator_ref[pl.ds(by, 8), :])
                    seconds.append(pattern * operator_ref[pl.ds(by + 8, 8), :])
                while len(firsts) > 1:
                    firsts = [m + n for m, n in zip(firsts[::2], firsts[1::2])]
                    seconds = [m + n for m, n in zip(seconds[::2], seconds[1::2])]
                return total + firsts[0], turned + seconds[0]

            steps = scalars[g * 4 + 1, 64 + b]
            total, turned = lax.fori_loop(0, steps, step, (zero, zero))
            out_ref[pl.ds(pl.multiple_of(g * 64 + b * 8, 8), 8), :] = (
                total + swap_parts(turned) * sign
            )
        return carry

    lax.fori_loop(0, groups, group, 0)


def disaggregate(get_row, boxes, cols, tiles, table, rows, first_row, sizes, store):
    fill_phases(table, rows, first_row, *sizes)
    weights = azimuth_weights(cols, True)
    sub, _ = tile_iota()
    sign = jnp.where(sub < 4, -1.0, 1.0).astype(jnp.float32)
    zero = jnp.zeros((8, LANES), jnp.float32)

    def shift(b, carry):
        plain = [get_row(i, b) for i in range(len(rows))]
        turned = [swap_parts(tile) * sign for tile in plain]
        for p in range(4):
            sums = []
            for which, source in enumerate((plain, turned)):
                product = []
                for i in range(len(rows)):
                    at = (i * 4 + p) * 16 + which * 8
                    product.append(source[i] * table[at : at + 8, :])
                per_row = []
                for k in range(8):
                    terms = [
                        (TAP[r - 2 * k], product[i]) for i, r in enumerate(rows) if r - 2 * k in TAP
                    ]
                    per_row.append(weighted(terms) if terms else None)
                sums.append(per_row)
            for k in range(8):
                for c, scale in ((4 + p, 1.0), (3 - p, -1.0)):
                    if sums[0][k] is None:
                        tile = zero
                    else:
                        tile = sums[0][k] + sums[1][k] if scale > 0 else sums[0][k] - sums[1][k]
                    at = pl.multiple_of(b * 512 + (c * 8 + k) * 8, 8)
                    tiles[pl.ds(at, 8), :] = tile
        return carry

    lax.fori_loop(0, boxes, shift, 0)

    def gather(b, carry):
        even, odd = [], []
        for part in range(2):
            blocks = [tiles[pl.ds(b * 512 + part * 4 + block, 64, stride=8), :] for block in range(4)]
            even.append(jnp.concatenate(blocks[:2], axis=1))
            odd.append(jnp.concatenate(blocks[2:], axis=1))
        mixed = split_dot(jnp.concatenate(odd, axis=0), weights)
        for part in range(2):
            store(part, b, even[part] + mixed[part * 64 : part * 64 + 64])
        return carry

    lax.fori_loop(0, boxes, gather, 0)


def inner_kernel(sizes, r_ref, out_ref, tiles, table):
    def get_row(i, b):
        return r_ref[pl.ds(pl.multiple_of(i * 64 + b * 8, 8), 8), :]

    def store(part, b, value):
        out_ref[part, pl.ds(pl.multiple_of(b * 64, 8), 64), :] = value

    first_row = lax.axis_index("dir") * 16
    boxes, cols = out_ref.shape[1] // 64, out_ref.shape[2]
    rows = tuple(range(16))
    disaggregate(get_row, boxes, cols, tiles, table, rows, first_row, sizes, store)


def outer_kernel(sizes, before_ref, after_ref, part_ref, out_ref, tiles, table):
    def get_row(i, b):
        ref = before_ref if i < HALO else after_ref
        return ref[pl.ds(pl.multiple_of((i % HALO) * 64 + b * 8, 8), 8), :]

    def store(part, b, value):
        at = pl.ds(pl.multiple_of(b * 64, 8), 64)
        out_ref[part, at, :] = part_ref[part, at, :] + value

    first_row = lax.axis_index("dir") * 16
    boxes, cols = out_ref.shape[1] // 64, out_ref.shape[2]
    rows = (-3, -2, -1, 16, 17, 18)
    disaggregate(get_row, boxes, cols, tiles, table, rows, first_row, sizes, store)


def neighbours(upward, downward):
    size = lax.axis_size("dir")
    to_next = [(i, i + 1) for i in range(size - 1)]
    to_last = [(i + 1, i) for i in range(size - 1)]
    return lax.ppermute(upward, "dir", to_next), lax.ppermute(downward, "dir", to_last)


def call(kernel, outs, scratch, flops, moved, *args):
    return pl.pallas_call(
        kernel,
        out_shape=outs,
        scratch_shapes=scratch,
        compiler_params=pltpu.CompilerParams(vmem_limit_bytes=VMEM),
        cost_estimate=pl.CostEstimate(flops=flops, bytes_accessed=moved, transcendentals=0),
    )(*args)


def list_notes(source_list, operator_list, operators):
    boxes = source_list.shape[0]
    used = source_list >= 0
    at = jnp.where(used, (source_list + source_list // boxes) * 8, 0)
    by = jnp.where(used, operator_list, operators) * 16
    steps = (jnp.sum(used.astype(jnp.int32), axis=1) + CHUNK - 1) // CHUNK
    at = jnp.concatenate([at.reshape(-1), steps, jnp.zeros((56,), jnp.int32)])
    by = jnp.concatenate([by.reshape(-1), jnp.zeros((64,), jnp.int32)])
    notes = jnp.concatenate([at, by, jnp.zeros((512,), jnp.int32)])
    return notes.reshape(8, LANES).astype(jnp.float32)


def on_device(child_patterns, translation, source_list, operator_list):
    parts, boxes, kids, half_rows, cols = child_patterns.shape
    local_rows = 2 * half_rows
    sizes = (local_rows * lax.axis_size("dir"), 2 * cols)
    groups = lax.axis_size("box")
    operators = translation.shape[0]
    f32 = jnp.float32
    shape = jax.ShapeDtypeStruct
    x = child_patterns.reshape(parts, boxes * kids * half_rows, cols)
    work = pltpu.VMEM((boxes * 512, LANES), f32)

    def phase_table(rows):
        return pltpu.VMEM((rows * 64, LANES), f32)

    up, down = call(
        functools.partial(halo_kernel, *sizes),
        [shape((HALO * boxes * 8, LANES), f32)] * 2,
        [work, phase_table(2 * HALO)],
        10**7,
        10**6,
        x,
    )
    before, after = neighbours(down, up)
    notes = list_notes(source_list, operator_list, operators)
    row = lax.dynamic_index_in_dim(translation, lax.axis_index("box"), 2, keepdims=False)
    row = row.reshape(operators * 2, 2 * cols)
    own, sorted_operators = call(
        functools.partial(main_kernel, *sizes),
        [
            shape((local_rows * 72, LANES), f32),
            shape(((operators + 1) * 16, LANES), f32),
        ],
        [work, phase_table(local_rows)],
        2 * 10**7,
        4 * 10**6,
        x,
        notes,
        row,
    )
    own = own.reshape(local_rows, 72, LANES)
    extra = ((0, 0), (0, 8), (0, 0))
    before = jnp.pad(before.reshape(HALO, 64, LANES), extra)
    after = jnp.pad(after.reshape(HALO, 64, LANES), extra)
    parent = jnp.concatenate([own[:HALO] + before, own[HALO:-HALO], own[-HALO:] + after])
    patterns = lax.all_to_all(parent, "box", 0, 0, tiled=True)
    received = call(
        translate_kernel,
        shape((groups * 64, LANES), f32),
        [
            pltpu.VMEM((groups * 4, LANES), jnp.int32),
            pltpu.SMEM((groups * 4, LANES), jnp.int32),
            pltpu.SemaphoreType.DMA,
        ],
        2 * 10**7,
        2 * 10**6,
        patterns.reshape(groups * 72, LANES),
        sorted_operators,
    )
    received = received.reshape(groups, 64, LANES)
    received = lax.all_to_all(received, "box", 0, 0, tiled=True)
    received = received.reshape(local_rows * 64, LANES)
    edge = HALO * 64
    before, after = neighbours(received[-edge:], received[:edge])
    out_shape = shape((parts, boxes * kids * half_rows, cols), f32)
    inner = call(
        functools.partial(inner_kernel, sizes),
        out_shape,
        [work, phase_table(local_rows)],
        2 * 10**7,
        4 * 10**6,
        received,
    )
    out = call(
        functools.partial(outer_kernel, sizes),
        out_shape,
        [work, phase_table(2 * HALO)],
        10**7,
        2 * 10**6,
        before,
        after,
        inner,
    )
    return out.reshape(child_patterns.shape)


def solution(mesh):
    return jax.shard_map(
        on_device,
        mesh=mesh,
        in_specs=(
            P(None, "box", None, "dir", None),
            P(None, None, "dir", None),
            P("box", None),
            P("box", None),
        ),
        out_specs=P(None, "box", None, "dir", None),
        check_vma=False,
    )
```

time: 325 us -> 98.3 us (0.30)
  waiting for transfers between devices: 162 us -> 0.67 us
  matrix products: 76.1 us -> 0 us
  blocking collectives: 0 us -> 51.8 us
  other arithmetic: 30.9 us -> 2.71 us
  Pallas kernels: 0 us -> 25.7 us
  local copies, waits for them, and re-layouts: 21.1 us -> 3.74 us
  starting transfers between devices: 30.2 us -> 12.9 us
    ppermute x19 -> x4, waiting for transfers between devices: 162 us -> 0.67 us  [the longest x2 0.66 us: neighbours(): lax.ppermute(downward, 'dir', to_last)]
    dot_general x36 -> x0, matrix products: 76.1 us -> none  [the longest x16 57.1 us: add_range(): jnp.einsum('dsn,ncrp->dscrp', counts, translation, precision=lax.Precisio...]
    all_to_all x0 -> x2, blocking collectives: none -> 51.8 us  [the longest x1 30.9 us: on_device(): patterns = lax.all_to_all(parent, 'box', 0, 0, tiled=True)]
    reduce_sum x17 -> x0, other arithmetic: 25.8 us -> none  [the longest x16 25.2 us: add_range(): jnp.sum(weights[:, :, 0] * patterns_in[0][None] - weights[:, :, 1] * patt...]
    pallas_call x0 -> x5, Pallas kernels: none -> 25.7 us  [call(): pl.pallas_call(kernel, out_shape=outs, scratch_shapes=scratch, compiler_p...]
    ppermute x19 -> x4, starting transfers between devices: 30.2 us -> 12.9 us  [the longest x2 8.43 us: neighbours(): lax.ppermute(upward, 'dir', to_next)]
    while x15 -> x0, local copies, waits for them, and re-layouts: 11.9 us -> none
  transfers between devices with their start and end apart: 19 -> 4, of which waited for: 17 -> 1; matrix products, arithmetic and copies ran while one was open for 21% -> 4% of each run, Pallas kernels for 0% -> 7%
where the time goes in v1:
time: 98.3 us; the launch traced here: 97.7 us
  blocking collectives  51.8 us (53%)
  Pallas kernels  25.7 us (26%)
  starting transfers between devices  12.9 us (13%)
  local copies, waits for them, and re-layouts  3.74 us (4%)
  other arithmetic  2.71 us (3%)
    all_to_all x1, blocking collectives, on_device(): patterns = lax.all_to_all(parent, 'box', 0, 0, tiled=True)  30.9 us
    pallas_call x5, Pallas kernels, call(): pl.pallas_call(kernel, out_shape=outs, scratch_shapes=scratch, compiler_p...  25.7 us
    all_to_all x1, blocking collectives, on_device(): received = lax.all_to_all(received, 'box', 0, 0, tiled=True)  20.9 us
    ppermute x2, starting transfers between devices, neighbours(): lax.ppermute(upward, 'dir', to_next)  8.43 us
    ppermute x2, starting transfers between devices, neighbours(): lax.ppermute(downward, 'dir', to_last)  4.47 us
  transfers between devices with their start and end apart: 4, of which 1 were waited for; matrix products, arithmetic and copies ran while one was open for 4% of the time, Pallas kernels for 7%

profile of v1, /device:TPU:1, one launch (start us, length us, event | category | flops | bytes accessed | tf_op | source)
XLA Modules:
  0.0 97.7 jit_solution(17400883685486592563)
XLA Ops:
  0.0 0.0 copy-start
  0.0 0.0 copy-start.1
  0.0 1.4 %copy-done.1 = f32[2,8,8,8,256]{4,3,2,1,0:T(8,128)S(1)} copy-done((f32[2,8,8,8,256]{4,3,2,1,0:T(8,128)S(1)}, f32[2,8,8,8,256]{4,3,2,1,0:T(8,128)}, u32[]{:S(2)}) %copy-start.1) | copy-done | bytes 1048600
  1.4 0.0 copy-start.2
  1.4 2.2 %shard_map.47 = (f32[192,128]{1,0:T(8,128)S(1)}, f32[192,128]{1,0:T(8,128)S(1)}) custom-call(f32[2,512,256]{2,1,0:T(8,128)S(1)} %bitcast.14), custom_call_target="tpu_custom_call" | custom-call | flops 10000000 | bytes 1000000 | tf_op jit(solution)/shard_map/pallas_call | solution.py:329
  3.6 4.5 %collective-permute-start = (f32[192,128]{1,0:T(8,128)S(1)}, f32[192,128]{1,0:T(8,128)}, u32[]{:S(2)}, u32[]{:S(2)}) collective-permute-start(f32[192,128]{1,0:T(8,128)S(1)} %get-tuple-element.10), channel_id=1, source_target_pairs={{0,16},{16,32},{32,48},{48,64},{64,80},{80,96},{96,112},{112,128},... | collective-permute-start | bytes 294920 | tf_op jit(solution)/shard_map/ppermute | solution.py:325
  8.1 2.5 %collective-permute-start.1 = (f32[192,128]{1,0:T(8,128)S(1)}, f32[192,128]{1,0:T(8,128)}, u32[]{:S(2)}, u32[]{:S(2)}) collective-permute-start(f32[192,128]{1,0:T(8,128)S(1)} %get-tuple-element.11), channel_id=1, source_target_pairs={{16,0},{32,16},{48,32},{64,48},{80,64},{96,80},{112,96},{128,112},... | collective-permute-start | bytes 294920 | tf_op jit(solution)/shard_map/ppermute | solution.py:325
  10.6 0.8 select_multiply_fusion
  11.5 0.1 reshape.41
  11.6 0.1 reshape.40
  11.6 0.1 concatenate.6
  11.7 0.0 copy-done
  11.7 1.1 %dynamic-slice_reduce_fusion = f32[32,2,512]{2,1,0:T(2,128)} fusion(f32[32,2,16,512]{3,2,1,0:T(8,128)S(1)} %copy-done, s32[]{:T(128)S(6)} %select_n.25), kind=kLoop, calls=%fused_computation.1 | loop fusion | bytes 262148 | tf_op jit(solution)/shard_map/jit(dynamic_index_in_dim)/dynamic_slice | solution.py:374
  12.8 1.0 %reshape.42.row_ref = f32[64,512]{1,0:T(8,128)S(1)} reshape(f32[32,2,512]{2,1,0:T(2,128)} %dynamic-slice_reduce_fusion) | data formatting | bytes 262144 | tf_op jit(solution)/shard_map/reshape | solution.py:375
  13.8 0.0 copy-done.2
  13.8 3.5 %shard_map.46 = (f32[1152,128]{1,0:T(8,128)S(1)}, f32[528,128]{1,0:T(8,128)S(1)}) custom-call(f32[2,512,256]{2,1,0:T(8,128)S(1)} %bitcast.15, f32[8,128]{1,0:T(8,128)S(1)} %convert_bitcast_fusion.note_ref, f32[64,512]{1,0:T(8,128)S(1)} %reshape.42.row_ref), custom_call_target="tpu_custom_call" | custom-call | flops 20000000 | bytes 4000000 | tf_op jit(solution)/shard_map/pallas_call | solution.py:329
  17.4 0.0 collective-permute-done
  17.4 0.9 pad_add_fusion.1
  18.3 0.0 collective-permute-done.1
  18.4 0.9 pad_add_fusion
  19.3 30.9 %all_to_all.10 = f32[16,72,128]{2,1,0:T(8,128)S(1)} all-to-all(f32[16,72,128]{2,1,0:T(8,128)S(1)} %pad_maximum_fusion), channel_id=1, replica_groups=mesh['dir'=16,'box'=16] {'box'}, dimensions={0} | all-to-all | bytes 1179648 | tf_op jit(solution)/shard_map/all_to_all | solution.py:394
  50.2 13.5 %shard_map.48 = f32[1024,128]{1,0:T(8,128)S(1)} custom-call(f32[1152,128]{1,0:T(8,128)S(1)} %bitcast.17, f32[528,128]{1,0:T(8,128)S(1)} %get-tuple-element.12.operator_ref), custom_call_target="tpu_custom_call" | custom-call | flops 20000000 | bytes 2000000 | tf_op jit(solution)/shard_map/pallas_call | solution.py:329
  63.7 20.9 %all_to_all.11 = f32[16,64,128]{2,1,0:T(8,128)S(1)} all-to-all(f32[16,64,128]{2,1,0:T(8,128)S(1)} %bitcast.18), channel_id=1, replica_groups=mesh['dir'=16,'box'=16] {'box'}, dimensions={0} | all-to-all | bytes 1048576 | tf_op jit(solution)/shard_map/all_to_all | solution.py:409
  84.7 3.9 %collective-permute-start.2 = (f32[192,128]{1,0:T(8,128)S(1)}, f32[192,128]{1,0:T(8,128)S(1)}, u32[]{:S(2)}, u32[]{:S(2)}) collective-permute-start(f32[192,128]{1,0:T(8,128)S(1)} %bitcast.23), channel_id=1, source_target_pairs={{0,16},{16,32},{32,48},{48,64},{64,80},{80,96},{96,112},{112,128},... | collective-permute-start | bytes 294920 | tf_op jit(solution)/shard_map/ppermute | solution.py:325
  88.6 1.9 %collective-permute-start.3 = (f32[192,128]{1,0:T(8,128)S(1)}, f32[192,128]{1,0:T(8,128)S(1)}, u32[]{:S(2)}, u32[]{:S(2)}) collective-permute-start(f32[192,128]{1,0:T(8,128)S(1)} %bitcast.22), channel_id=1, source_target_pairs={{16,0},{32,16},{48,32},{64,48},{80,64},{96,80},{112,96},{128,112},... | collective-permute-start | bytes 294920 | tf_op jit(solution)/shard_map/ppermute | solution.py:325
  90.6 3.3 %shard_map.49.part_ref = f32[2,512,256]{2,1,0:T(8,128)S(1)} custom-call(f32[1024,128]{1,0:T(8,128)S(1)} %bitcast.16), custom_call_target="tpu_custom_call" | custom-call | flops 20000000 | bytes 4000000 | tf_op jit(solution)/shard_map/pallas_call | solution.py:329
  93.9 0.0 collective-permute-done.2.before_ref
  93.9 0.7 collective-permute-done.3.after_ref
  94.6 3.2 %shard_map.50 = f32[2,512,256]{2,1,0:T(8,128)} custom-call(f32[192,128]{1,0:T(8,128)S(1)} %collective-permute-done.2.before_ref, f32[192,128]{1,0:T(8,128)S(1)} %collective-permute-done.3.after_ref, f32[2,512,256]{2,1,0:T(8,128)S(1)} %shard_map.49.part_ref), custom_call_target="tpu_custom_call" | custom-call | flops 10000000 | bytes 2000000 | tf_op jit(solution)/shard_map/pallas_call | solution.py:329
  (9 shorter events, 0.1 us)
Async XLA Ops:
  0.0 11.7 %copy-start = (f32[32,2,16,512]{3,2,1,0:T(8,128)S(1)}, f32[32,2,16,512]{3,2,1,0:T(8,128)}, u32[]{:S(2)}) copy-start(f32[32,2,16,512]{3,2,1,0:T(8,128)} %param.5) | copy-start | bytes 6291460
  0.0 1.4 %copy-start.1 = (f32[2,8,8,8,256]{4,3,2,1,0:T(8,128)S(1)}, f32[2,8,8,8,256]{4,3,2,1,0:T(8,128)}, u32[]{:S(2)}) copy-start(f32[2,8,8,8,256]{4,3,2,1,0:T(8,128)} %param.4) | copy-start | bytes 3145732
  1.4 12.4 %copy-start.2 = (f32[2,8,8,8,256]{4,3,2,1,0:T(8,128)S(1)}, f32[2,8,8,8,256]{4,3,2,1,0:T(8,128)}, u32[]{:S(2)}) copy-start(f32[2,8,8,8,256]{4,3,2,1,0:T(8,128)} %param.4) | copy-start | bytes 3145732
  3.6 13.9 %collective-permute-start = (f32[192,128]{1,0:T(8,128)S(1)}, f32[192,128]{1,0:T(8,128)}, u32[]{:S(2)}, u32[]{:S(2)}) collective-permute-start(f32[192,128]{1,0:T(8,128)S(1)} %get-tuple-element.10), channel_id=1, source_target_pairs={{0,16},{16,32},{32,48},{48,64},{64,80},{80,96},{96,112},{112,128},... | collective-permute-start | bytes 294920 | tf_op jit(solution)/shard_map/ppermute | solution.py:325
  8.1 10.3 %collective-permute-start.1 = (f32[192,128]{1,0:T(8,128)S(1)}, f32[192,128]{1,0:T(8,128)}, u32[]{:S(2)}, u32[]{:S(2)}) collective-permute-start(f32[192,128]{1,0:T(8,128)S(1)} %get-tuple-element.11), channel_id=1, source_target_pairs={{16,0},{32,16},{48,32},{64,48},{80,64},{96,80},{112,96},{128,112},... | collective-permute-start | bytes 294920 | tf_op jit(solution)/shard_map/ppermute | solution.py:325
  84.7 9.2 %collective-permute-start.2 = (f32[192,128]{1,0:T(8,128)S(1)}, f32[192,128]{1,0:T(8,128)S(1)}, u32[]{:S(2)}, u32[]{:S(2)}) collective-permute-start(f32[192,128]{1,0:T(8,128)S(1)} %bitcast.23), channel_id=1, source_target_pairs={{0,16},{16,32},{32,48},{48,64},{64,80},{80,96},{96,112},{112,128},... | collective-permute-start | bytes 294920 | tf_op jit(solution)/shard_map/ppermute | solution.py:325
  88.6 5.9 %collective-permute-start.3 = (f32[192,128]{1,0:T(8,128)S(1)}, f32[192,128]{1,0:T(8,128)S(1)}, u32[]{:S(2)}, u32[]{:S(2)}) collective-permute-start(f32[192,128]{1,0:T(8,128)S(1)} %bitcast.22), channel_id=1, source_target_pairs={{16,0},{32,16},{48,32},{64,48},{80,64},{96,80},{112,96},{128,112},... | collective-permute-start | bytes 294920 | tf_op jit(solution)/shard_map/ppermute | solution.py:325

commit v2 on v1

v2 whole, which is shorter than its diff:
```python
import functools

import jax
import jax.numpy as jnp
from jax import lax
from jax.experimental import pallas as pl
from jax.experimental.pallas import tpu as pltpu
from jax.sharding import PartitionSpec as P

TAP = {
    -3: -0.0390625,
    -2: -0.0546875,
    -1: 0.2734375,
    0: 0.8203125,
    1: 0.8203125,
    2: 0.2734375,
    3: -0.0546875,
    4: -0.0390625,
}
KIDS = 8
HALO = 3
LANES = 128
OPERATORS = 32
MAIN_ROWS = tuple(range(-3, 13))
EDGE_ROWS = tuple(range(13, 19))
VMEM = 24 * 1024 * 1024
PICK_VMEM = 61_500_000


def tile_iota():
    sub = lax.broadcasted_iota(jnp.int32, (8, LANES), 0)
    lane = lax.broadcasted_iota(jnp.int32, (8, LANES), 1)
    return sub, lane


def swap_parts(tile):
    return jnp.concatenate([tile[4:8], tile[0:4]], axis=0)


def sin_cos(angle):
    quarter = jnp.floor(angle * (2.0 / jnp.pi) + 0.5)
    rest = angle - quarter * 1.5703125
    rest = rest - quarter * 4.837512969970703125e-4
    rest = rest - quarter * 7.54978995489188e-8
    square = rest * rest
    sine = -1.9515295891e-4 * square + 8.3321608736e-3
    sine = (sine * square - 1.6666654611e-1) * square * rest + rest
    cosine = 2.443315711809948e-5 * square - 1.388731625493765e-3
    cosine = (cosine * square + 4.166664568298827e-2) * square * square - 0.5 * square + 1.0
    number = quarter.astype(jnp.int32)
    odd = (number & 1) == 1
    first, second = jnp.where(odd, cosine, sine), jnp.where(odd, sine, cosine)
    first = jnp.where((number & 2) == 2, -first, first)
    second = jnp.where(((number + 1) & 2) == 2, -second, second)
    return first, second


def fill_phases(table, rows, first_row, total_rows, total_cols):
    sub, lane = tile_iota()
    block = sub % 4
    sample = 2 * ((block % 2) * LANES + lane) + block // 2
    azimuth = sample.astype(jnp.float32) * (2.0 * jnp.pi / total_cols)
    low = sub < 4
    sin_azimuth, cos_azimuth = sin_cos(azimuth)
    course = jnp.where(low, cos_azimuth, sin_azimuth)
    wave = 0.125 * total_rows
    padded = -(-len(rows) // 8) * 8
    number = lax.broadcasted_iota(jnp.int32, (padded, LANES), 0) + (first_row + rows[0])
    inside = (number >= 0) & (number < total_rows)
    polar = (number.astype(jnp.float32) + 0.5) * (jnp.pi / total_rows)
    sin_polar, cos_polar = sin_cos(polar)
    sin_z, cos_z = sin_cos(wave * cos_polar)
    sin_polar = wave * sin_polar
    cos_z, sin_z = jnp.where(inside, cos_z, 0.0), jnp.where(inside, sin_z, 0.0)
    for i in range(len(rows)):
        sin_a, cos_a = sin_cos(sin_polar[i : i + 1] * course)
        cos_b, sin_b = swap_parts(cos_a), swap_parts(sin_a)
        cx, cy = jnp.where(low, cos_a, cos_b), jnp.where(low, cos_b, cos_a)
        sx, sy = jnp.where(low, sin_a, sin_b), jnp.where(low, sin_b, sin_a)
        cc, ss, sc, cs = cx * cy, sx * sy, sx * cy, cx * sy
        plus_c, plus_s = cc - ss, sc + cs
        minus_c, minus_s = cc + ss, sc - cs
        cz, sz = cos_z[i : i + 1], sin_z[i : i + 1]
        for p in range(4):
            x_up, y_up = p % 2 == 1, p // 2 == 1
            base_c, base_s = (plus_c, plus_s) if x_up == y_up else (minus_c, minus_s)
            if not x_up:
                base_s = -base_s
            at = (i * 4 + p) * 16
            table[at : at + 8, :] = base_c * cz - base_s * sz
            table[at + 8 : at + 16, :] = base_s * cz + base_c * sz


def azimuth_weights(cols, transpose):
    i = lax.broadcasted_iota(jnp.int32, (cols, cols), 0)
    j = lax.broadcasted_iota(jnp.int32, (cols, cols), 1)
    shift = (j - i if transpose else i - j) % cols
    near = (shift == 0) | (shift == 1)
    far = (shift == cols - 1) | (shift == 2)
    return jnp.where(near, 0.5625, jnp.where(far, -0.0625, 0.0)).astype(jnp.bfloat16)


def split_dot(values, weights):
    high = values.astype(jnp.bfloat16)
    rest = (values - high.astype(jnp.float32)).astype(jnp.bfloat16)
    both = jnp.concatenate([high, rest], axis=0)
    out = jnp.dot(both, weights, preferred_element_type=jnp.float32)
    count = values.shape[0]
    return out[:count] + out[count:]


def weighted(terms):
    total = None
    for coef, tile in terms:
        part = coef * tile
        total = part if total is None else total + part
    return total


def aggregate(x_ref, tiles, table, rows, store):
    boxes = x_ref.shape[1] // 64
    weights = azimuth_weights(x_ref.shape[2], False)
    sub, _ = tile_iota()
    sign = jnp.where(sub < 4, 1.0, -1.0).astype(jnp.float32)

    def refine(b):
        parts = []
        for part in range(2):
            kids = [x_ref[part, pl.ds(pl.multiple_of(b * 64 + c * 8, 8), 8), :] for c in range(KIDS)]
            both = [kids[4 + p] + kids[3 - p] for p in range(4)]
            both += [kids[4 + p] - kids[3 - p] for p in range(4)]
            parts.append(jnp.concatenate(both, axis=0))
        even = jnp.concatenate(parts, axis=0)
        odd = split_dot(even, weights)
        for part in range(2):
            for block in range(4):
                source = even if block < 2 else odd
                lanes = slice((block % 2) * LANES, (block % 2 + 1) * LANES)
                tiles[pl.ds(b * 512 + part * 4 + block, 64, stride=8), :] = source[
                    part * 64 : part * 64 + 64, lanes
                ]

    def combine(b):
        for i, r in enumerate(rows):
            taps = [(TAP[r - 2 * k], k) for k in range(8) if r - 2 * k in TAP]
            total, turned = None, None
            for p in range(4):
                sums = []
                for q in (p, 4 + p):
                    parts = []
                    for coef, k in taps:
                        at = pl.multiple_of(b * 512 + (q * 8 + k) * 8, 8)
                        parts.append((coef, tiles[pl.ds(at, 8), :]))
                    sums.append(weighted(parts))
                at = (i * 4 + p) * 16
                first = sums[0] * table[at : at + 8, :]
                second = sums[1] * table[at + 8 : at + 16, :]
                total = first if total is None else total + first
                turned = second if turned is None else turned + second
            store(i, b, total + swap_parts(turned) * sign)

    def box(b, carry):
        refine(b)
        combine(b)
        return carry

    lax.fori_loop(0, boxes, box, 0, unroll=2)


def edge_kernel(sizes, x_ref, out_ref, table, tiles):
    fill_phases(table, EDGE_ROWS, lax.axis_index("dir") * 16, *sizes)

    def store(i, b, tile):
        out_ref[pl.ds(pl.multiple_of(i * 64 + b * 8, 8), 8), :] = tile

    aggregate(x_ref, tiles, table, EDGE_ROWS, store)


def main_kernel(sizes, x_ref, source_ref, list_ref, out_ref, table, tiles):
    fill_phases(table, MAIN_ROWS, lax.axis_index("dir") * 16, *sizes)

    def store(i, b, tile):
        out_ref[pl.ds(pl.multiple_of(i * 72 + b * 8, 8), 8), :] = tile

    aggregate(x_ref, tiles, table, MAIN_ROWS, store)
    boxes, entries = source_ref.shape
    source = source_ref[...]
    used = source >= 0
    at = jnp.where(used, (source + source // boxes) * 8, 0)
    by = jnp.where(used, list_ref[...], OPERATORS) * 16
    out_ref[64:72, :] = jnp.zeros((8, LANES), jnp.float32)
    out_ref[64:72, 0:entries] = at.astype(jnp.float32)
    out_ref[64:72, 32 : 32 + entries] = by.astype(jnp.float32)
    note = out_ref[64:72, :]
    for r in range(1, len(MAIN_ROWS)):
        out_ref[r * 72 + 64 : r * 72 + 72, :] = note


def join_kernel(own_ref, edge_ref, out_ref):
    count = len(EDGE_ROWS)
    for i in range(count):
        out_ref[i * 72 : i * 72 + 64, :] = (
            own_ref[i * 72 : i * 72 + 64, :] + edge_ref[i * 64 : i * 64 + 64, :]
        )
        out_ref[i * 72 + 64 : i * 72 + 72, :] = own_ref[i * 72 + 64 : i * 72 + 72, :]
    out_ref[count * 72 :, :] = own_ref[count * 72 :, :]


def pick_kernel(all_ref, out_ref, block_ref, sem):
    rows = all_ref.shape[1]
    wanted = (lax.axis_index("box") + rows - HALO) % rows
    near = pl.ds(pl.multiple_of(wanted // 8 * 8, 8), 8)
    copy = pltpu.make_async_copy(all_ref.at[:, near, :], block_ref, sem)
    copy.start()
    copy.wait()
    at = wanted % 8

    def eight(i, carry):
        first = pl.multiple_of(i * 8, 8)
        rows = [block_ref[first + n, pl.ds(at, 1), :] for n in range(8)]
        out_ref[pl.ds(first, 8), :] = jnp.concatenate(rows, axis=0)
        return carry

    lax.fori_loop(0, out_ref.shape[0] // 8, eight, 0)


def sort_kernel(row_ref, out_ref):
    count, wide = row_ref.shape
    source = lax.broadcasted_iota(jnp.int32, (wide, wide), 0)
    target = lax.broadcasted_iota(jnp.int32, (wide, wide), 1)
    half = wide // 2
    wanted = jnp.where(target < half, 2 * target, 2 * (target - half) + 1)
    pick = jnp.where(source == wanted, 1.0, 0.0).astype(jnp.bfloat16)
    values = row_ref[...]
    high = values.astype(jnp.bfloat16)
    rest = values - high.astype(jnp.float32)
    middle = rest.astype(jnp.bfloat16)
    low = (rest - middle.astype(jnp.float32)).astype(jnp.bfloat16)
    three = jnp.dot(
        jnp.concatenate([high, middle, low], axis=0), pick, preferred_element_type=jnp.float32
    )
    in_order = three[:count] + three[count : 2 * count] + three[2 * count :]
    for block in range(4):
        part = in_order[:, block * LANES : (block + 1) * LANES]
        out_ref[pl.ds(block, count, stride=8), :] = part
        out_ref[pl.ds(block + 4, count, stride=8), :] = part
    out_ref[count * 8 : count * 8 + 16, :] = jnp.zeros((16, LANES), jnp.float32)


def translate_kernel(entries, x_ref, operator_ref, out_ref, notes, scalars, sems):
    pairs = out_ref.shape[0] // 128
    sub, lane = tile_iota()
    for h in range(pairs):
        at = h * 144 + 64
        first, second = x_ref[at : at + 8, :], x_ref[at + 72 : at + 80, :]
        both = jnp.where(lane < 64, first, pltpu.roll(second, 64, 1))
        notes[h * 8 : h * 8 + 8, :] = both.astype(jnp.int32)

    def copy(h):
        at = pl.ds(h * 8, 8)
        return pltpu.make_async_copy(notes.at[at, :], scalars.at[at, :], sems.at[h])

    for h in range(pairs):
        copy(h).start()
    sign = jnp.where(sub < 4, -1.0, 1.0).astype(jnp.float32)

    for h in range(pairs):
        copy(h).wait()
        for g in range(2):
            for base in (0, 4):
                sums = [[None, None] for _ in range(4)]
                for k in range(entries):
                    for j in range(4):
                        row = h * 8 + base + j
                        at = pl.multiple_of(scalars[row, g * 64 + k], 8)
                        by = pl.multiple_of(scalars[row, g * 64 + 32 + k], 8)
                        pattern = x_ref[pl.ds(at, 8), :]
                        for which in range(2):
                            part = pattern * operator_ref[pl.ds(by + 8 * which, 8), :]
                            total = sums[j][which]
                            sums[j][which] = part if total is None else total + part
                for j in range(4):
                    at = h * 128 + g * 64 + (base + j) * 8
                    out_ref[at : at + 8, :] = sums[j][0] + swap_parts(sums[j][1]) * sign


def shift_sums(b, get_row, table, rows, kids, sign, put):
    plain = [get_row(i, b) for i in range(len(rows))]
    turned = [swap_parts(tile) * sign for tile in plain]
    for p in range(4):
        sums = []
        for which, source in enumerate((plain, turned)):
            product = []
            for i in range(len(rows)):
                at = (i * 4 + p) * 16 + which * 8
                product.append(source[i] * table[at : at + 8, :])
            per_row = []
            for k in kids:
                terms = [(TAP[r - 2 * k], product[i]) for i, r in enumerate(rows) if r - 2 * k in TAP]
                per_row.append(weighted(terms))
            sums.append(per_row)
        for n, k in enumerate(kids):
            put(4 + p, k, sums[0][n] + sums[1][n])
            put(3 - p, k, sums[0][n] - sums[1][n])


def turn_sign():
    sub, _ = tile_iota()
    return jnp.where(sub < 4, -1.0, 1.0).astype(jnp.float32)


def azimuth_back(tiles, base, rows, weights):
    even, odd = [], []
    for part in range(2):
        blocks = [tiles[pl.ds(base + part * 4 + block, rows, stride=8), :] for block in range(4)]
        even.append(jnp.concatenate(blocks[:2], axis=1))
        odd.append(jnp.concatenate(blocks[2:], axis=1))
    mixed = split_dot(jnp.concatenate(odd, axis=0), weights)
    return [even[part] + mixed[part * rows : part * rows + rows] for part in range(2)]


def inner_kernel(r_ref, table, out_ref, tiles):
    boxes, cols = out_ref.shape[1] // 64, out_ref.shape[2]
    weights = azimuth_weights(cols, True)
    sign = turn_sign()

    def get_row(i, b):
        return r_ref[pl.ds(pl.multiple_of(i * 64 + b * 8, 8), 8), :]

    def shift(b, carry):
        def put(c, k, tile):
            tiles[pl.ds(pl.multiple_of(b * 512 + (c * 8 + k) * 8, 8), 8), :] = tile

        shift_sums(b, get_row, table, MAIN_ROWS, tuple(range(8)), sign, put)
        values = azimuth_back(tiles, b * 512, 64, weights)
        for part in range(2):
            out_ref[part, pl.ds(pl.multiple_of(b * 64, 64), 64), :] = values[part]
        return carry

    lax.fori_loop(0, boxes, shift, 0, unroll=2)


def outer_kernel(edge_ref, table, part_ref, out_hbm, out_ref, tiles, sems):
    boxes, cols = out_ref.shape[1] // 64, out_ref.shape[2]
    weights = azimuth_weights(cols, True)
    sign = turn_sign()
    nothing = jnp.zeros((8, LANES), jnp.float32)

    def get_row(i, b):
        return edge_ref[pl.ds(pl.multiple_of(i * 64 + b * 8, 8), 8), :]

    def copy(part, b):
        at = pl.ds(pl.multiple_of(b * 64, 64), 64)
        return pltpu.make_async_copy(
            out_ref.at[part, at, :], out_hbm.at[part, at, :], sems.at[part, b]
        )

    blank = jnp.zeros((4, cols), jnp.float32)

    def box(b, carry):
        def put(c, k, tile):
            tiles[pl.ds(pl.multiple_of(b * 256 + (c * 4 + k - 4) * 8, 8), 8), :] = tile

        for c in range(KIDS):
            put(c, 4, nothing)
        shift_sums(b, get_row, table, EDGE_ROWS, (5, 6, 7), sign, put)
        values = azimuth_back(tiles, b * 256, 32, weights)
        at = pl.ds(pl.multiple_of(b * 64, 64), 64)
        for part in range(2):
            pieces = []
            for c in range(KIDS):
                pieces += [blank, values[part][c * 4 : c * 4 + 4]]
            out_ref[part, at, :] = part_ref[part, at, :] + jnp.concatenate(pieces, axis=0)
            copy(part, b).start()
        return carry

    lax.fori_loop(0, boxes, box, 0, unroll=2)
    for b in range(boxes):
        for part in range(2):
            copy(part, b).wait()


def to_next(value, step):
    size = lax.axis_size("dir")
    return lax.ppermute(value, "dir", [(i, (i + step) % size) for i in range(size)])


def call(kernel, outs, scratch, flops, moved, *args, in_hbm=(), out_hbm=False, limit=VMEM):
    whole = pl.BlockSpec(memory_space=pltpu.VMEM)
    far = pl.BlockSpec(memory_space=pltpu.HBM)
    out_specs = [whole] * len(outs) if isinstance(outs, list) else far if out_hbm else whole
    return pl.pallas_call(
        kernel,
        out_shape=outs,
        in_specs=[far if i in in_hbm else whole for i in range(len(args))],
        out_specs=out_specs,
        scratch_shapes=scratch,
        compiler_params=pltpu.CompilerParams(vmem_limit_bytes=limit),
        cost_estimate=pl.CostEstimate(flops=flops, bytes_accessed=moved, transcendentals=0),
    )(*args)


def on_device(child_patterns, translation, source_list, operator_list):
    parts, boxes, kids, half_rows, cols = child_patterns.shape
    local_rows = 2 * half_rows
    sizes = (local_rows * lax.axis_size("dir"), 2 * cols)
    groups = lax.axis_size("box")
    operators = translation.shape[0]
    f32 = jnp.float32
    shape = jax.ShapeDtypeStruct
    x = child_patterns.reshape(parts, boxes * kids * half_rows, cols)
    work = pltpu.VMEM((boxes * 512, LANES), f32)
    sems = pltpu.SemaphoreType.DMA((parts, boxes))
    edge = len(EDGE_ROWS)

    share, edge_table = call(
        functools.partial(edge_kernel, sizes),
        [shape((edge * boxes * 8, LANES), f32), shape((edge * 64, LANES), f32)],
        [work],
        10**7,
        10**6,
        x,
    )
    from_last = to_next(share, 1)
    own, main_table = call(
        functools.partial(main_kernel, sizes),
        [shape((local_rows * 72, LANES), f32), shape((local_rows * 64, LANES), f32)],
        [work],
        2 * 10**7,
        4 * 10**6,
        x,
        source_list,
        operator_list,
    )
    parent = call(join_kernel, shape(own.shape, f32), [], 10**5, 10**6, own, from_last)

    parent, translation = lax.optimization_barrier((parent, translation))
    place = lax.axis_index("box")
    row = call(
        pick_kernel,
        shape((operators * 2, 2 * cols), f32),
        [pltpu.VMEM((operators * 2, 8, 2 * cols), f32), pltpu.SemaphoreType.DMA],
        2 * 10**7,
        4 * 10**6,
        translation.reshape(operators * 2, local_rows, 2 * cols),
        in_hbm=(0,),
        limit=PICK_VMEM,
    )
    row = jnp.where(place < HALO, to_next(row, 1), row)
    sorted_operators = call(
        sort_kernel, shape(((operators + 1) * 16, LANES), f32), [], 2 * 10**7, 4 * 10**6, row
    )
    patterns = lax.all_to_all(
        parent.reshape(local_rows, 72, LANES), "box", 0, 0, tiled=True
    ).reshape(groups * 72, LANES)
    received = call(
        functools.partial(translate_kernel, source_list.shape[1]),
        shape((groups * 64, LANES), f32),
        [
            pltpu.VMEM((groups * 4, LANES), jnp.int32),
            pltpu.SMEM((groups * 4, LANES), jnp.int32),
            pltpu.SemaphoreType.DMA((groups // 2,)),
        ],
        2 * 10**7,
        2 * 10**6,
        patterns,
        sorted_operators,
    )
    received = received.reshape(groups, 64, LANES)
    received = lax.all_to_all(received, "box", 0, 0, tiled=True)
    received = received.reshape(local_rows * 64, LANES)
    from_next = to_next(received[: edge * 64], -1)
    inner = call(
        inner_kernel, shape(x.shape, f32), [work], 2 * 10**7, 4 * 10**6, received, main_table
    )
    out = call(
        outer_kernel,
        shape(x.shape, f32),
        [pltpu.VMEM(x.shape, f32), pltpu.VMEM((boxes * 256, LANES), f32), sems],
        10**7,
        2 * 10**6,
        from_next,
        edge_table,
        inner,
        out_hbm=True,
    )
    return out.reshape(child_patterns.shape)


def solution(mesh):
    return jax.shard_map(
        on_device,
        mesh=mesh,
        in_specs=(
            P(None, "box", None, "dir", None),
            P(None, None, "dir", None),
            P("box", None),
            P("box", None),
        ),
        out_specs=P(None, "box", None, "dir", None),
        check_vma=False,
    )
```

time: 98.3 us -> 74.8 us (0.76)
  blocking collectives: 51.8 us -> 18.2 us
  waiting for transfers between devices: 0.67 us -> 17.8 us
  Pallas kernels: 25.7 us -> 15.4 us
  starting transfers between devices: 12.9 us -> 20.4 us
  other arithmetic: 2.71 us -> 0.02 us
  local copies, waits for them, and re-layouts: 3.74 us -> 2.61 us
    all_to_all x1 -> x0, blocking collectives: 30.9 us -> none  [on_device(): patterns = lax.all_to_all(parent, 'box', 0, 0, tiled=True)]
    all_to_all x0 -> x1, waiting for transfers between devices: none -> 11.1 us  [on_device(): lax.all_to_all(parent.reshape(local_rows, 72, LANES), 'box', 0, 0, tiled=...]
    all_to_all x0 -> x1, starting transfers between devices: none -> 10.9 us  [on_device(): lax.all_to_all(parent.reshape(local_rows, 72, LANES), 'box', 0, 0, tiled=...]
    pallas_call x5 -> x8, Pallas kernels: 25.7 us -> 15.4 us  [call(): pl.pallas_call(kernel, out_shape=outs, in_specs=[far if i in in_hbm else...]
    ppermute x4 -> x3, waiting for transfers between devices: 0.67 us -> 6.72 us  [to_next(): lax.ppermute(value, 'dir', [(i, (i + step) % size) for i in range(size)])]
    ppermute x4 -> x3, starting transfers between devices: 12.9 us -> 9.44 us  [to_next(): lax.ppermute(value, 'dir', [(i, (i + step) % size) for i in range(size)])]
    all_to_all x1, blocking collectives: 20.9 us -> 18.2 us  [on_device(): received = lax.all_to_all(received, 'box', 0, 0, tiled=True)]
    add x2 -> x0, other arithmetic: 1.83 us -> none  [the longest x1 0.92 us: on_device(): own[-HALO:] + after]
  transfers between devices with their start and end apart: 4 -> 4, of which waited for: 1 -> 3; matrix products, arithmetic and copies ran while one was open for 4% -> 0% of each run, Pallas kernels for 7% -> 9%
where the time goes in v2:
time: 74.8 us; the launch traced here: 74.4 us
  starting transfers between devices  20.4 us (27%)
  blocking collectives  18.2 us (24%)
  waiting for transfers between devices  17.8 us (24%)
  Pallas kernels  15.4 us (21%)
  local copies, waits for them, and re-layouts  2.61 us (3%)
    all_to_all x1, blocking collectives, on_device(): received = lax.all_to_all(received, 'box', 0, 0, tiled=True)  18.2 us
    pallas_call x8, Pallas kernels, call(): pl.pallas_call(kernel, out_shape=outs, in_specs=[far if i in in_hbm else...  15.4 us
    all_to_all x1, waiting for transfers between devices, on_device(): lax.all_to_all(parent.reshape(local_rows, 72, LANES), 'box', 0, 0, tiled=...  11.1 us
    all_to_all x1, starting transfers between devices, on_device(): lax.all_to_all(parent.reshape(local_rows, 72, LANES), 'box', 0, 0, tiled=...  10.9 us
    ppermute x3, starting transfers between devices, to_next(): lax.ppermute(value, 'dir', [(i, (i + step) % size) for i in range(size)])  9.44 us
    ppermute x3, waiting for transfers between devices, to_next(): lax.ppermute(value, 'dir', [(i, (i + step) % size) for i in range(size)])  6.72 us
    unnamed x6, local copies, waits for them, and re-layouts  2.6 us
  transfers between devices with their start and end apart: 4, of which 3 were waited for; matrix products, arithmetic and copies ran while one was open for 0% of the time, Pallas kernels for 9%

profile of v2, /device:TPU:1, one launch (start us, length us, event | category | flops | bytes accessed | tf_op | source)
XLA Modules:
  0.0 74.4 jit_solution(6209469378025200076)
XLA Ops:
  0.0 0.0 copy-start
  0.0 1.2 %copy-done = f32[2,8,8,8,256]{4,3,2,1,0:T(8,128)S(1)} copy-done((f32[2,8,8,8,256]{4,3,2,1,0:T(8,128)S(1)}, f32[2,8,8,8,256]{4,3,2,1,0:T(8,128)}, u32[]{:S(2)}) %copy-start) | copy-done | bytes 1048600
  1.2 1.4 %shard_map.47 = (f32[384,128]{1,0:T(8,128)S(1)}, f32[384,128]{1,0:T(8,128)S(1)}) custom-call(f32[2,512,256]{2,1,0:T(8,128)S(1)} %bitcast.8), custom_call_target="tpu_custom_call" | custom-call | flops 10000000 | bytes 1000000 | tf_op jit(solution)/shard_map/pallas_call | solution.py:392
  2.6 2.7 %collective-permute-start = (f32[384,128]{1,0:T(8,128)S(1)}, f32[384,128]{1,0:T(8,128)S(1)}, u32[]{:S(2)}, u32[]{:S(2)}) collective-permute-start(f32[384,128]{1,0:T(8,128)S(1)} %get-tuple-element.12), channel_id=1, source_target_pairs={{0,16},{16,32},{32,48},{48,64},{64,80},{80,96},{96,112},{112,128},... | collective-permute-start | bytes 589832 | tf_op jit(solution)/shard_map/ppermute | solution.py:385
  5.3 0.0 copy-start.1
  5.3 0.7 copy-done.1
  6.0 0.0 copy-start.2
  6.0 0.7 copy-done.2
  6.7 2.3 %shard_map.46 = (f32[1152,128]{1,0:T(8,128)S(1)}, f32[1024,128]{1,0:T(8,128)S(1)}) custom-call(f32[2,512,256]{2,1,0:T(8,128)S(1)} %bitcast.9, s32[8,24]{1,0:T(8,128)S(1)} %copy-done.1, s32[8,24]{1,0:T(8,128)S(1)} %copy-done.2), custom_call_target="tpu_custom_call" | custom-call | flops 20000000 | bytes 4000000 | tf_op jit(solution)/shard_map/pallas_call | solution.py:392
  9.0 0.0 collective-permute-done.edge_ref
  9.1 0.9 %shard_map.48 = f32[1152,128]{1,0:T(8,128)} custom-call(f32[1152,128]{1,0:T(8,128)S(1)} %get-tuple-element.11.own_ref, f32[384,128]{1,0:T(8,128)S(1)} %collective-permute-done.edge_ref), custom_call_target="tpu_custom_call" | custom-call | flops 100000 | bytes 1000000 | tf_op jit(solution)/shard_map/pallas_call | solution.py:392
  9.9 10.9 %all-to-all-start = ((f32[16,72,128]{2,1,0:T(8,128)}), f32[16,72,128]{2,1,0:T(8,128)S(1)}, u32[]{:S(2)}, u32[]{:S(2)}) async-start(f32[16,72,128]{2,1,0:T(8,128)} %bitcast.1), calls=%async_computation | async-start | bytes 1179648 | tf_op jit(solution)/shard_map/all_to_all | solution.py:453
  20.9 2.0 %shard_map.49 = f32[64,512]{1,0:T(8,128)} custom-call(f32[64,16,512]{2,1,0:T(8,128)} %bitcast.13), custom_call_target="tpu_custom_call" | custom-call | flops 20000000 | bytes 4000000 | tf_op jit(solution)/shard_map/pallas_call | solution.py:392
  22.9 1.7 %collective-permute-start.1 = (f32[64,512]{1,0:T(8,128)}, f32[64,512]{1,0:T(8,128)S(1)}, u32[]{:S(2)}, u32[]{:S(2)}) collective-permute-start(f32[64,512]{1,0:T(8,128)} %shard_map.49), channel_id=1, source_target_pairs={{0,16},{16,32},{32,48},{48,64},{64,80},{80,96},{96,112},{112,128},... | collective-permute-start | bytes 393224 | tf_op jit(solution)/shard_map/ppermute | solution.py:385
  24.6 2.3 %collective-permute-done.1 = f32[64,512]{1,0:T(8,128)S(1)} collective-permute-done((f32[64,512]{1,0:T(8,128)}, f32[64,512]{1,0:T(8,128)S(1)}, u32[]{:S(2)}, u32[]{:S(2)}) %collective-permute-start.1) | collective-permute-done | bytes 131104 | tf_op jit(solution)/shard_map/ppermute | solution.py:385
  26.9 0.3 shard_map.50.operator_ref
  27.2 11.1 %all-to-all-done = f32[16,72,128]{2,1,0:T(8,128)S(1)} async-done(((f32[16,72,128]{2,1,0:T(8,128)}), f32[16,72,128]{2,1,0:T(8,128)S(1)}, u32[]{:S(2)}, u32[]{:S(2)}) %all-to-all-start) | async-done | bytes 589856 | tf_op jit(solution)/shard_map/all_to_all | solution.py:453
  38.3 4.2 %shard_map.51 = f32[1024,128]{1,0:T(8,128)S(1)} custom-call(f32[1152,128]{1,0:T(8,128)S(1)} %bitcast.11, f32[528,128]{1,0:T(8,128)S(1)} %shard_map.50.operator_ref), custom_call_target="tpu_custom_call" | custom-call | flops 20000000 | bytes 2000000 | tf_op jit(solution)/shard_map/pallas_call | solution.py:392
  42.5 18.2 %all_to_all.10 = f32[16,64,128]{2,1,0:T(8,128)S(1)} all-to-all(f32[16,64,128]{2,1,0:T(8,128)S(1)} %bitcast.12), channel_id=1, replica_groups=mesh['dir'=16,'box'=16] {'box'}, dimensions={0} | all-to-all | bytes 1048576 | tf_op jit(solution)/shard_map/all_to_all | solution.py:470
  60.7 5.1 %collective-permute-start.2 = (f32[384,128]{1,0:T(8,128)S(1)}, f32[384,128]{1,0:T(8,128)S(1)}, u32[]{:S(2)}, u32[]{:S(2)}) collective-permute-start(f32[384,128]{1,0:T(8,128)S(1)} %bitcast.14), channel_id=1, source_target_pairs={{0,240},{16,0},{32,16},{48,32},{64,48},{80,64},{96,80},{112,96},{1... | collective-permute-start | bytes 589832 | tf_op jit(solution)/shard_map/ppermute | solution.py:385
  65.8 2.2 %shard_map.52.part_ref = f32[2,512,256]{2,1,0:T(8,128)S(1)} custom-call(f32[1024,128]{1,0:T(8,128)S(1)} %bitcast.10, f32[1024,128]{1,0:T(8,128)S(1)} %get-tuple-element.16.table), custom_call_target="tpu_custom_call" | custom-call | flops 20000000 | bytes 4000000 | tf_op jit(solution)/shard_map/pallas_call | solution.py:392
  68.0 4.5 %collective-permute-done.2.edge_ref = f32[384,128]{1,0:T(8,128)S(1)} collective-permute-done((f32[384,128]{1,0:T(8,128)S(1)}, f32[384,128]{1,0:T(8,128)S(1)}, u32[]{:S(2)}, u32[]{:S(2)}) %collective-permute-start.2) | collective-permute-done | bytes 196640 | tf_op jit(solution)/shard_map/ppermute | solution.py:385
  72.4 2.0 %shard_map.53 = f32[2,512,256]{2,1,0:T(8,128)} custom-call(f32[384,128]{1,0:T(8,128)S(1)} %collective-permute-done.2.edge_ref, f32[384,128]{1,0:T(8,128)S(1)} %get-tuple-element.15.table, f32[2,512,256]{2,1,0:T(8,128)S(1)} %shard_map.52.part_ref), custom_call_target="tpu_custom_call" | custom-call | flops 10000000 | bytes 2000000 | tf_op jit(solution)/shard_map/pallas_call | solution.py:392
  (2 shorter events, 0.0 us)
Async XLA Ops:
  0.0 1.2 %copy-start = (f32[2,8,8,8,256]{4,3,2,1,0:T(8,128)S(1)}, f32[2,8,8,8,256]{4,3,2,1,0:T(8,128)}, u32[]{:S(2)}) copy-start(f32[2,8,8,8,256]{4,3,2,1,0:T(8,128)} %param.4) | copy-start | bytes 3145732
  2.6 6.4 %collective-permute-start = (f32[384,128]{1,0:T(8,128)S(1)}, f32[384,128]{1,0:T(8,128)S(1)}, u32[]{:S(2)}, u32[]{:S(2)}) collective-permute-start(f32[384,128]{1,0:T(8,128)S(1)} %get-tuple-element.12), channel_id=1, source_target_pairs={{0,16},{16,32},{32,48},{48,64},{64,80},{80,96},{96,112},{112,128},... | collective-permute-start | bytes 589832 | tf_op jit(solution)/shard_map/ppermute | solution.py:385
  5.3 0.7 copy-start.1
  6.0 0.7 copy-start.2
  9.9 28.4 %all-to-all-start = ((f32[16,72,128]{2,1,0:T(8,128)}), f32[16,72,128]{2,1,0:T(8,128)S(1)}, u32[]{:S(2)}, u32[]{:S(2)}) async-start(f32[16,72,128]{2,1,0:T(8,128)} %bitcast.1), calls=%async_computation | async-start | bytes 1179648 | tf_op jit(solution)/shard_map/all_to_all | solution.py:453
  22.9 4.0 %collective-permute-start.1 = (f32[64,512]{1,0:T(8,128)}, f32[64,512]{1,0:T(8,128)S(1)}, u32[]{:S(2)}, u32[]{:S(2)}) collective-permute-start(f32[64,512]{1,0:T(8,128)} %shard_map.49), channel_id=1, source_target_pairs={{0,16},{16,32},{32,48},{48,64},{64,80},{80,96},{96,112},{112,128},... | collective-permute-start | bytes 393224 | tf_op jit(solution)/shard_map/ppermute | solution.py:385
  60.7 11.7 %collective-permute-start.2 = (f32[384,128]{1,0:T(8,128)S(1)}, f32[384,128]{1,0:T(8,128)S(1)}, u32[]{:S(2)}, u32[]{:S(2)}) collective-permute-start(f32[384,128]{1,0:T(8,128)S(1)} %bitcast.14), channel_id=1, source_target_pairs={{0,240},{16,0},{32,16},{48,32},{64,48},{80,64},{96,80},{112,96},{1... | collective-permute-start | bytes 589832 | tf_op jit(solution)/shard_map/ppermute | solution.py:385

commit v3 on v2

--- a/solution.py
+++ b/solution.py
@@ -164,10 +164,10 @@
         combine(b)
         return carry
 
-    lax.fori_loop(0, boxes, box, 0, unroll=2)
-
-
-def edge_kernel(sizes, x_ref, out_ref, table, tiles):
+    lax.fori_loop(0, boxes, box, 0, unroll=4)
+
+
+def edge_kernel(sizes, x_ref, out_ref, table, same_ref, tiles):
     fill_phases(table, EDGE_ROWS, lax.axis_index("dir") * 16, *sizes)
 
     def store(i, b, tile):
@@ -176,18 +176,18 @@
     aggregate(x_ref, tiles, table, EDGE_ROWS, store)
 
 
-def main_kernel(sizes, x_ref, source_ref, list_ref, out_ref, table, tiles):
+def main_kernel(sizes, x_ref, lists_ref, out_ref, table, tiles):
     fill_phases(table, MAIN_ROWS, lax.axis_index("dir") * 16, *sizes)
 
     def store(i, b, tile):
         out_ref[pl.ds(pl.multiple_of(i * 72 + b * 8, 8), 8), :] = tile
 
     aggregate(x_ref, tiles, table, MAIN_ROWS, store)
-    boxes, entries = source_ref.shape
-    source = source_ref[...]
+    boxes, entries = lists_ref.shape[0] // 2, lists_ref.shape[1]
+    source = lists_ref[:boxes, :]
     used = source >= 0
     at = jnp.where(used, (source + source // boxes) * 8, 0)
-    by = jnp.where(used, list_ref[...], OPERATORS) * 16
+    by = jnp.where(used, lists_ref[boxes:, :], OPERATORS) * 16
     out_ref[64:72, :] = jnp.zeros((8, LANES), jnp.float32)
     out_ref[64:72, 0:entries] = at.astype(jnp.float32)
     out_ref[64:72, 32 : 32 + entries] = by.astype(jnp.float32)
@@ -374,7 +374,7 @@
             copy(part, b).start()
         return carry
 
-    lax.fori_loop(0, boxes, box, 0, unroll=2)
+    lax.fori_loop(0, boxes, box, 0, unroll=4)
     for b in range(boxes):
         for part in range(2):
             copy(part, b).wait()
@@ -385,7 +385,7 @@
     return lax.ppermute(value, "dir", [(i, (i + step) % size) for i in range(size)])
 
 
-def call(kernel, outs, scratch, flops, moved, *args, in_hbm=(), out_hbm=False, limit=VMEM):
+def call(kernel, outs, scratch, flops, moved, *args, in_hbm=(), out_hbm=False, limit=VMEM, aliases=None):
     whole = pl.BlockSpec(memory_space=pltpu.VMEM)
     far = pl.BlockSpec(memory_space=pltpu.HBM)
     out_specs = [whole] * len(outs) if isinstance(outs, list) else far if out_hbm else whole
@@ -395,6 +395,7 @@
         in_specs=[far if i in in_hbm else whole for i in range(len(args))],
         out_specs=out_specs,
         scratch_shapes=scratch,
+        input_output_aliases=aliases or {},
         compiler_params=pltpu.CompilerParams(vmem_limit_bytes=limit),
         cost_estimate=pl.CostEstimate(flops=flops, bytes_accessed=moved, transcendentals=0),
     )(*args)
@@ -413,13 +414,21 @@
     sems = pltpu.SemaphoreType.DMA((parts, boxes))
     edge = len(EDGE_ROWS)
 
-    share, edge_table = call(
+    share, edge_table, x = call(
         functools.partial(edge_kernel, sizes),
-        [shape((edge * boxes * 8, LANES), f32), shape((edge * 64, LANES), f32)],
+        [
+            shape((edge * boxes * 8, LANES), f32),
+            shape((edge * 64, LANES), f32),
+            shape(x.shape, f32),
+        ],
         [work],
         10**7,
         10**6,
         x,
+        aliases={0: 2},
+    )
+    share, source_list, operator_list = lax.optimization_barrier(
+        (share, source_list, operator_list)
     )
     from_last = to_next(share, 1)
     own, main_table = call(
@@ -429,8 +438,7 @@
         2 * 10**7,
         4 * 10**6,
         x,
-        source_list,
-        operator_list,
+        jnp.concatenate([source_list, operator_list]),
     )
     parent = call(join_kernel, shape(own.shape, f32), [], 10**5, 10**6, own, from_last)
 

time: 74.8 us -> 72.5 us (0.969)
  starting transfers between devices: 20.4 us -> 22.8 us
  waiting for transfers between devices: 17.8 us -> 15.7 us
  local copies, waits for them, and re-layouts: 2.61 us -> 1.27 us
  Pallas kernels: 15.4 us -> 14.3 us
    all_to_all x1, waiting for transfers between devices: 11.1 us -> 8.26 us  [on_device(): lax.all_to_all(parent.reshape(local_rows, 72, LANES), 'box', 0, 0, tiled=...]
    ppermute x3, starting transfers between devices: 9.44 us -> 11.9 us  [to_next(): lax.ppermute(value, 'dir', [(i, (i + step) % size) for i in range(size)])]
    unnamed x6 -> x5, local copies, waits for them, and re-layouts: 2.6 us -> 1.26 us
    pallas_call x8, Pallas kernels: 15.4 us -> 14.3 us  [call(): pl.pallas_call(kernel, out_shape=outs, in_specs=[far if i in in_hbm else...]
    ppermute x3, waiting for transfers between devices: 6.72 us -> 7.48 us  [to_next(): lax.ppermute(value, 'dir', [(i, (i + step) % size) for i in range(size)])]
  transfers between devices with their start and end apart: 4 -> 4, of which waited for: 3 -> 4; matrix products, arithmetic and copies ran while one was open for 0% -> 0% of each run, Pallas kernels for 9% -> 9%
where the time goes in v3:
time: 72.5 us; the launch traced here: 72.2 us
  starting transfers between devices  22.8 us (31%)
  blocking collectives  18 us (25%)
  waiting for transfers between devices  15.7 us (22%)
  Pallas kernels  14.3 us (20%)
  local copies, waits for them, and re-layouts  1.27 us (2%)
    all_to_all x1, blocking collectives, on_device(): received = lax.all_to_all(received, 'box', 0, 0, tiled=True)  18 us
    pallas_call x8, Pallas kernels, call(): pl.pallas_call(kernel, out_shape=outs, in_specs=[far if i in in_hbm else...  14.3 us
    ppermute x3, starting transfers between devices, to_next(): lax.ppermute(value, 'dir', [(i, (i + step) % size) for i in range(size)])  11.9 us
    all_to_all x1, starting transfers between devices, on_device(): lax.all_to_all(parent.reshape(local_rows, 72, LANES), 'box', 0, 0, tiled=...  10.9 us
    all_to_all x1, waiting for transfers between devices, on_device(): lax.all_to_all(parent.reshape(local_rows, 72, LANES), 'box', 0, 0, tiled=...  8.26 us
    ppermute x3, waiting for transfers between devices, to_next(): lax.ppermute(value, 'dir', [(i, (i + step) % size) for i in range(size)])  7.48 us
  transfers between devices with their start and end apart: 4, of which 4 were waited for; matrix products, arithmetic and copies ran while one was open for 0% of the time, Pallas kernels for 9%

profile of v3, /device:TPU:1, one launch (start us, length us, event | category | flops | bytes accessed | tf_op | source)
XLA Modules:
  0.0 72.2 jit_solution(12789297183009045162)
XLA Ops:
  0.0 0.0 copy-start.1
  0.0 0.0 copy-start
  0.0 1.3 %copy.8 = f32[2,8,8,8,256]{4,3,2,1,0:T(8,128)S(1)} copy(f32[2,8,8,8,256]{4,3,2,1,0:T(8,128)} %param.4) | data formatting | bytes 2097152
  1.3 1.0 %shard_map.46 = (f32[384,128]{1,0:T(8,128)S(1)}, f32[384,128]{1,0:T(8,128)S(1)}, f32[2,512,256]{2,1,0:T(8,128)S(1)}) custom-call(f32[2,512,256]{2,1,0:T(8,128)S(1)} %bitcast.8), custom_call_target="tpu_custom_call", output_to_operand_aliasing={{2}: (0, {})} | custom-call | flops 10000000 | bytes 1000000 | tf_op jit(solution)/shard_map/pallas_call | solution.py:392
  2.3 2.7 %collective-permute-start = (f32[384,128]{1,0:T(8,128)S(1)}, f32[384,128]{1,0:T(8,128)S(1)}, u32[]{:S(2)}, u32[]{:S(2)}) collective-permute-start(f32[384,128]{1,0:T(8,128)S(1)} %get-tuple-element.20), channel_id=1, source_target_pairs={{0,16},{16,32},{32,48},{48,64},{64,80},{80,96},{96,112},{112,128},... | collective-permute-start | bytes 589832 | tf_op jit(solution)/shard_map/ppermute | solution.py:385
  5.0 0.0 copy-done.1
  5.0 0.0 copy-done
  5.0 2.0 %shard_map.47 = (f32[1152,128]{1,0:T(8,128)S(1)}, f32[1024,128]{1,0:T(8,128)S(1)}) custom-call(f32[2,512,256]{2,1,0:T(8,128)S(1)} %get-tuple-element.15.x_ref, s32[16,24]{1,0:T(8,128)S(1)} %pad_add_fusion.lists_ref), custom_call_target="tpu_custom_call" | custom-call | flops 20000000 | bytes 4000000 | tf_op jit(solution)/shard_map/pallas_call | solution.py:392
  7.0 0.6 collective-permute-done.edge_ref
  7.6 0.9 %shard_map.48 = f32[1152,128]{1,0:T(8,128)} custom-call(f32[1152,128]{1,0:T(8,128)S(1)} %get-tuple-element.19.own_ref, f32[384,128]{1,0:T(8,128)S(1)} %collective-permute-done.edge_ref), custom_call_target="tpu_custom_call" | custom-call | flops 100000 | bytes 1000000 | tf_op jit(solution)/shard_map/pallas_call | solution.py:392
  8.5 10.9 %all-to-all-start = ((f32[16,72,128]{2,1,0:T(8,128)}), f32[16,72,128]{2,1,0:T(8,128)S(1)}, u32[]{:S(2)}, u32[]{:S(2)}) async-start(f32[16,72,128]{2,1,0:T(8,128)} %bitcast.1), calls=%async_computation | async-start | bytes 1179648 | tf_op jit(solution)/shard_map/all_to_all | solution.py:461
  19.4 2.0 %shard_map.49 = f32[64,512]{1,0:T(8,128)} custom-call(f32[64,16,512]{2,1,0:T(8,128)} %bitcast.12), custom_call_target="tpu_custom_call" | custom-call | flops 20000000 | bytes 4000000 | tf_op jit(solution)/shard_map/pallas_call | solution.py:392
  21.4 2.8 %collective-permute-start.1 = (f32[64,512]{1,0:T(8,128)}, f32[64,512]{1,0:T(8,128)S(1)}, u32[]{:S(2)}, u32[]{:S(2)}) collective-permute-start(f32[64,512]{1,0:T(8,128)} %shard_map.49), channel_id=1, source_target_pairs={{0,16},{16,32},{32,48},{48,64},{64,80},{80,96},{96,112},{112,128},... | collective-permute-start | bytes 393224 | tf_op jit(solution)/shard_map/ppermute | solution.py:385
  24.2 2.3 %collective-permute-done.1 = f32[64,512]{1,0:T(8,128)S(1)} collective-permute-done((f32[64,512]{1,0:T(8,128)}, f32[64,512]{1,0:T(8,128)S(1)}, u32[]{:S(2)}, u32[]{:S(2)}) %collective-permute-start.1) | collective-permute-done | bytes 131104 | tf_op jit(solution)/shard_map/ppermute | solution.py:385
  26.5 0.3 shard_map.50.operator_ref
  26.8 8.3 %all-to-all-done = f32[16,72,128]{2,1,0:T(8,128)S(1)} async-done(((f32[16,72,128]{2,1,0:T(8,128)}), f32[16,72,128]{2,1,0:T(8,128)S(1)}, u32[]{:S(2)}, u32[]{:S(2)}) %all-to-all-start) | async-done | bytes 589856 | tf_op jit(solution)/shard_map/all_to_all | solution.py:461
  35.1 4.2 %shard_map.51 = f32[1024,128]{1,0:T(8,128)S(1)} custom-call(f32[1152,128]{1,0:T(8,128)S(1)} %bitcast.10, f32[528,128]{1,0:T(8,128)S(1)} %shard_map.50.operator_ref), custom_call_target="tpu_custom_call" | custom-call | flops 20000000 | bytes 2000000 | tf_op jit(solution)/shard_map/pallas_call | solution.py:392
  39.3 18.0 %all_to_all.10 = f32[16,64,128]{2,1,0:T(8,128)S(1)} all-to-all(f32[16,64,128]{2,1,0:T(8,128)S(1)} %bitcast.11), channel_id=1, replica_groups=mesh['dir'=16,'box'=16] {'box'}, dimensions={0} | all-to-all | bytes 1048576 | tf_op jit(solution)/shard_map/all_to_all | solution.py:478
  57.3 6.4 %collective-permute-start.2 = (f32[384,128]{1,0:T(8,128)S(1)}, f32[384,128]{1,0:T(8,128)S(1)}, u32[]{:S(2)}, u32[]{:S(2)}) collective-permute-start(f32[384,128]{1,0:T(8,128)S(1)} %bitcast.13), channel_id=1, source_target_pairs={{0,240},{16,0},{32,16},{48,32},{64,48},{80,64},{96,80},{112,96},{1... | collective-permute-start | bytes 589832 | tf_op jit(solution)/shard_map/ppermute | solution.py:385
  63.7 2.2 %shard_map.52.part_ref = f32[2,512,256]{2,1,0:T(8,128)S(1)} custom-call(f32[1024,128]{1,0:T(8,128)S(1)} %bitcast.9, f32[1024,128]{1,0:T(8,128)S(1)} %get-tuple-element.24.table), custom_call_target="tpu_custom_call" | custom-call | flops 20000000 | bytes 4000000 | tf_op jit(solution)/shard_map/pallas_call | solution.py:392
  65.9 4.6 %collective-permute-done.2.edge_ref = f32[384,128]{1,0:T(8,128)S(1)} collective-permute-done((f32[384,128]{1,0:T(8,128)S(1)}, f32[384,128]{1,0:T(8,128)S(1)}, u32[]{:S(2)}, u32[]{:S(2)}) %collective-permute-start.2) | collective-permute-done | bytes 196640 | tf_op jit(solution)/shard_map/ppermute | solution.py:385
  70.5 1.7 %shard_map.53 = f32[2,512,256]{2,1,0:T(8,128)} custom-call(f32[384,128]{1,0:T(8,128)S(1)} %collective-permute-done.2.edge_ref, f32[384,128]{1,0:T(8,128)S(1)} %get-tuple-element.23.table, f32[2,512,256]{2,1,0:T(8,128)S(1)} %shard_map.52.part_ref), custom_call_target="tpu_custom_call" | custom-call | flops 10000000 | bytes 2000000 | tf_op jit(solution)/shard_map/pallas_call | solution.py:392
  (3 shorter events, 0.0 us)
Async XLA Ops:
  0.0 5.0 %copy-start.1 = (s32[8,24]{1,0:T(8,128)S(1)}, s32[8,24]{1,0:T(8,128)}, u32[]{:S(2)}) copy-start(s32[8,24]{1,0:T(8,128)} %param.6) | copy-start | bytes 2308
  0.0 5.0 %copy-start = (s32[8,24]{1,0:T(8,128)S(1)}, s32[8,24]{1,0:T(8,128)}, u32[]{:S(2)}) copy-start(s32[8,24]{1,0:T(8,128)} %param.7) | copy-start | bytes 2308
  2.3 5.3 %collective-permute-start = (f32[384,128]{1,0:T(8,128)S(1)}, f32[384,128]{1,0:T(8,128)S(1)}, u32[]{:S(2)}, u32[]{:S(2)}) collective-permute-start(f32[384,128]{1,0:T(8,128)S(1)} %get-tuple-element.20), channel_id=1, source_target_pairs={{0,16},{16,32},{32,48},{48,64},{64,80},{80,96},{96,112},{112,128},... | collective-permute-start | bytes 589832 | tf_op jit(solution)/shard_map/ppermute | solution.py:385
  8.5 26.6 %all-to-all-start = ((f32[16,72,128]{2,1,0:T(8,128)}), f32[16,72,128]{2,1,0:T(8,128)S(1)}, u32[]{:S(2)}, u32[]{:S(2)}) async-start(f32[16,72,128]{2,1,0:T(8,128)} %bitcast.1), calls=%async_computation | async-start | bytes 1179648 | tf_op jit(solution)/shard_map/all_to_all | solution.py:461
  21.4 5.1 %collective-permute-start.1 = (f32[64,512]{1,0:T(8,128)}, f32[64,512]{1,0:T(8,128)S(1)}, u32[]{:S(2)}, u32[]{:S(2)}) collective-permute-start(f32[64,512]{1,0:T(8,128)} %shard_map.49), channel_id=1, source_target_pairs={{0,16},{16,32},{32,48},{48,64},{64,80},{80,96},{96,112},{112,128},... | collective-permute-start | bytes 393224 | tf_op jit(solution)/shard_map/ppermute | solution.py:385
  57.3 13.2 %collective-permute-start.2 = (f32[384,128]{1,0:T(8,128)S(1)}, f32[384,128]{1,0:T(8,128)S(1)}, u32[]{:S(2)}, u32[]{:S(2)}) collective-permute-start(f32[384,128]{1,0:T(8,128)S(1)} %bitcast.13), channel_id=1, source_target_pairs={{0,240},{16,0},{32,16},{48,32},{64,48},{80,64},{96,80},{112,96},{1... | collective-permute-start | bytes 589832 | tf_op jit(solution)/shard_map/ppermute | solution.py:385

commit v4 on v3

--- a/solution.py
+++ b/solution.py
@@ -164,7 +164,7 @@
         combine(b)
         return carry
 
-    lax.fori_loop(0, boxes, box, 0, unroll=4)
+    lax.fori_loop(0, boxes, box, 0, unroll=8)
 
 
 def edge_kernel(sizes, x_ref, out_ref, table, same_ref, tiles):
@@ -374,7 +374,7 @@
             copy(part, b).start()
         return carry
 
-    lax.fori_loop(0, boxes, box, 0, unroll=4)
+    lax.fori_loop(0, boxes, box, 0, unroll=8)
     for b in range(boxes):
         for part in range(2):
             copy(part, b).wait()

time: 72.5 us -> 72.2 us (level)
  no operation moved by 1% of the time
where the time goes in v4:
time: 72.2 us; the launch traced here: 71.9 us
  starting transfers between devices  22.8 us (32%)
  blocking collectives  18 us (25%)
  waiting for transfers between devices  16 us (22%)
  Pallas kernels  13.8 us (19%)
  local copies, waits for them, and re-layouts  1.27 us (2%)
    all_to_all x1, blocking collectives, on_device(): received = lax.all_to_all(received, 'box', 0, 0, tiled=True)  18 us
    pallas_call x8, Pallas kernels, call(): pl.pallas_call(kernel, out_shape=outs, in_specs=[far if i in in_hbm else...  13.8 us
    ppermute x3, starting transfers between devices, to_next(): lax.ppermute(value, 'dir', [(i, (i + step) % size) for i in range(size)])  11.9 us
    all_to_all x1, starting transfers between devices, on_device(): lax.all_to_all(parent.reshape(local_rows, 72, LANES), 'box', 0, 0, tiled=...  10.9 us
    all_to_all x1, waiting for transfers between devices, on_device(): lax.all_to_all(parent.reshape(local_rows, 72, LANES), 'box', 0, 0, tiled=...  8.25 us
    ppermute x3, waiting for transfers between devices, to_next(): lax.ppermute(value, 'dir', [(i, (i + step) % size) for i in range(size)])  7.74 us
  transfers between devices with their start and end apart: 4, of which 4 were waited for; matrix products, arithmetic and copies ran while one was open for 0% of the time, Pallas kernels for 9%

profile of v4, /device:TPU:1, one launch (start us, length us, event | category | flops | bytes accessed | tf_op | source)
XLA Modules:
  0.0 71.9 jit_solution(8116953198735679563)
XLA Ops:
  0.0 0.0 copy-start.1
  0.0 0.0 copy-start
  0.0 1.3 %copy.8 = f32[2,8,8,8,256]{4,3,2,1,0:T(8,128)S(1)} copy(f32[2,8,8,8,256]{4,3,2,1,0:T(8,128)} %param.4) | data formatting | bytes 2097152
  1.3 0.8 %shard_map.46 = (f32[384,128]{1,0:T(8,128)S(1)}, f32[384,128]{1,0:T(8,128)S(1)}, f32[2,512,256]{2,1,0:T(8,128)S(1)}) custom-call(f32[2,512,256]{2,1,0:T(8,128)S(1)} %bitcast.8), custom_call_target="tpu_custom_call", output_to_operand_aliasing={{2}: (0, {})} | custom-call | flops 10000000 | bytes 1000000 | tf_op jit(solution)/shard_map/pallas_call | solution.py:392
  2.1 2.7 %collective-permute-start = (f32[384,128]{1,0:T(8,128)S(1)}, f32[384,128]{1,0:T(8,128)S(1)}, u32[]{:S(2)}, u32[]{:S(2)}) collective-permute-start(f32[384,128]{1,0:T(8,128)S(1)} %get-tuple-element.20), channel_id=1, source_target_pairs={{0,16},{16,32},{32,48},{48,64},{64,80},{80,96},{96,112},{112,128},... | collective-permute-start | bytes 589832 | tf_op jit(solution)/shard_map/ppermute | solution.py:385
  4.8 0.0 copy-done.1
  4.8 0.0 copy-done
  4.8 1.7 %shard_map.47 = (f32[1152,128]{1,0:T(8,128)S(1)}, f32[1024,128]{1,0:T(8,128)S(1)}) custom-call(f32[2,512,256]{2,1,0:T(8,128)S(1)} %get-tuple-element.15.x_ref, s32[16,24]{1,0:T(8,128)S(1)} %pad_add_fusion.lists_ref), custom_call_target="tpu_custom_call" | custom-call | flops 20000000 | bytes 4000000 | tf_op jit(solution)/shard_map/pallas_call | solution.py:392
  6.5 0.9 %collective-permute-done.edge_ref = f32[384,128]{1,0:T(8,128)S(1)} collective-permute-done((f32[384,128]{1,0:T(8,128)S(1)}, f32[384,128]{1,0:T(8,128)S(1)}, u32[]{:S(2)}, u32[]{:S(2)}) %collective-permute-start) | collective-permute-done | bytes 196640 | tf_op jit(solution)/shard_map/ppermute | solution.py:385
  7.4 0.9 %shard_map.48 = f32[1152,128]{1,0:T(8,128)} custom-call(f32[1152,128]{1,0:T(8,128)S(1)} %get-tuple-element.19.own_ref, f32[384,128]{1,0:T(8,128)S(1)} %collective-permute-done.edge_ref), custom_call_target="tpu_custom_call" | custom-call | flops 100000 | bytes 1000000 | tf_op jit(solution)/shard_map/pallas_call | solution.py:392
  8.2 10.9 %all-to-all-start = ((f32[16,72,128]{2,1,0:T(8,128)}), f32[16,72,128]{2,1,0:T(8,128)S(1)}, u32[]{:S(2)}, u32[]{:S(2)}) async-start(f32[16,72,128]{2,1,0:T(8,128)} %bitcast.1), calls=%async_computation | async-start | bytes 1179648 | tf_op jit(solution)/shard_map/all_to_all | solution.py:461
  19.2 2.0 %shard_map.49 = f32[64,512]{1,0:T(8,128)} custom-call(f32[64,16,512]{2,1,0:T(8,128)} %bitcast.12), custom_call_target="tpu_custom_call" | custom-call | flops 20000000 | bytes 4000000 | tf_op jit(solution)/shard_map/pallas_call | solution.py:392
  21.2 2.8 %collective-permute-start.1 = (f32[64,512]{1,0:T(8,128)}, f32[64,512]{1,0:T(8,128)S(1)}, u32[]{:S(2)}, u32[]{:S(2)}) collective-permute-start(f32[64,512]{1,0:T(8,128)} %shard_map.49), channel_id=1, source_target_pairs={{0,16},{16,32},{32,48},{48,64},{64,80},{80,96},{96,112},{112,128},... | collective-permute-start | bytes 393224 | tf_op jit(solution)/shard_map/ppermute | solution.py:385
  24.0 2.3 %collective-permute-done.1 = f32[64,512]{1,0:T(8,128)S(1)} collective-permute-done((f32[64,512]{1,0:T(8,128)}, f32[64,512]{1,0:T(8,128)S(1)}, u32[]{:S(2)}, u32[]{:S(2)}) %collective-permute-start.1) | collective-permute-done | bytes 131104 | tf_op jit(solution)/shard_map/ppermute | solution.py:385
  26.3 0.3 shard_map.50.operator_ref
  26.6 8.3 %all-to-all-done = f32[16,72,128]{2,1,0:T(8,128)S(1)} async-done(((f32[16,72,128]{2,1,0:T(8,128)}), f32[16,72,128]{2,1,0:T(8,128)S(1)}, u32[]{:S(2)}, u32[]{:S(2)}) %all-to-all-start) | async-done | bytes 589856 | tf_op jit(solution)/shard_map/all_to_all | solution.py:461
  34.9 4.2 %shard_map.51 = f32[1024,128]{1,0:T(8,128)S(1)} custom-call(f32[1152,128]{1,0:T(8,128)S(1)} %bitcast.10, f32[528,128]{1,0:T(8,128)S(1)} %shard_map.50.operator_ref), custom_call_target="tpu_custom_call" | custom-call | flops 20000000 | bytes 2000000 | tf_op jit(solution)/shard_map/pallas_call | solution.py:392
  39.1 18.0 %all_to_all.10 = f32[16,64,128]{2,1,0:T(8,128)S(1)} all-to-all(f32[16,64,128]{2,1,0:T(8,128)S(1)} %bitcast.11), channel_id=1, replica_groups=mesh['dir'=16,'box'=16] {'box'}, dimensions={0} | all-to-all | bytes 1048576 | tf_op jit(solution)/shard_map/all_to_all | solution.py:478
  57.1 6.4 %collective-permute-start.2 = (f32[384,128]{1,0:T(8,128)S(1)}, f32[384,128]{1,0:T(8,128)S(1)}, u32[]{:S(2)}, u32[]{:S(2)}) collective-permute-start(f32[384,128]{1,0:T(8,128)S(1)} %bitcast.13), channel_id=1, source_target_pairs={{0,240},{16,0},{32,16},{48,32},{64,48},{80,64},{96,80},{112,96},{1... | collective-permute-start | bytes 589832 | tf_op jit(solution)/shard_map/ppermute | solution.py:385
  63.5 2.2 %shard_map.52.part_ref = f32[2,512,256]{2,1,0:T(8,128)S(1)} custom-call(f32[1024,128]{1,0:T(8,128)S(1)} %bitcast.9, f32[1024,128]{1,0:T(8,128)S(1)} %get-tuple-element.24.table), custom_call_target="tpu_custom_call" | custom-call | flops 20000000 | bytes 4000000 | tf_op jit(solution)/shard_map/pallas_call | solution.py:392
  65.7 4.6 %collective-permute-done.2.edge_ref = f32[384,128]{1,0:T(8,128)S(1)} collective-permute-done((f32[384,128]{1,0:T(8,128)S(1)}, f32[384,128]{1,0:T(8,128)S(1)}, u32[]{:S(2)}, u32[]{:S(2)}) %collective-permute-start.2) | collective-permute-done | bytes 196640 | tf_op jit(solution)/shard_map/ppermute | solution.py:385
  70.2 1.7 %shard_map.53 = f32[2,512,256]{2,1,0:T(8,128)} custom-call(f32[384,128]{1,0:T(8,128)S(1)} %collective-permute-done.2.edge_ref, f32[384,128]{1,0:T(8,128)S(1)} %get-tuple-element.23.table, f32[2,512,256]{2,1,0:T(8,128)S(1)} %shard_map.52.part_ref), custom_call_target="tpu_custom_call" | custom-call | flops 10000000 | bytes 2000000 | tf_op jit(solution)/shard_map/pallas_call | solution.py:392
  (3 shorter events, 0.0 us)
Async XLA Ops:
  0.0 4.8 %copy-start.1 = (s32[8,24]{1,0:T(8,128)S(1)}, s32[8,24]{1,0:T(8,128)}, u32[]{:S(2)}) copy-start(s32[8,24]{1,0:T(8,128)} %param.6) | copy-start | bytes 2308
  0.0 4.8 %copy-start = (s32[8,24]{1,0:T(8,128)S(1)}, s32[8,24]{1,0:T(8,128)}, u32[]{:S(2)}) copy-start(s32[8,24]{1,0:T(8,128)} %param.7) | copy-start | bytes 2308
  2.1 5.3 %collective-permute-start = (f32[384,128]{1,0:T(8,128)S(1)}, f32[384,128]{1,0:T(8,128)S(1)}, u32[]{:S(2)}, u32[]{:S(2)}) collective-permute-start(f32[384,128]{1,0:T(8,128)S(1)} %get-tuple-element.20), channel_id=1, source_target_pairs={{0,16},{16,32},{32,48},{48,64},{64,80},{80,96},{96,112},{112,128},... | collective-permute-start | bytes 589832 | tf_op jit(solution)/shard_map/ppermute | solution.py:385
  8.2 26.6 %all-to-all-start = ((f32[16,72,128]{2,1,0:T(8,128)}), f32[16,72,128]{2,1,0:T(8,128)S(1)}, u32[]{:S(2)}, u32[]{:S(2)}) async-start(f32[16,72,128]{2,1,0:T(8,128)} %bitcast.1), calls=%async_computation | async-start | bytes 1179648 | tf_op jit(solution)/shard_map/all_to_all | solution.py:461
  21.2 5.1 %collective-permute-start.1 = (f32[64,512]{1,0:T(8,128)}, f32[64,512]{1,0:T(8,128)S(1)}, u32[]{:S(2)}, u32[]{:S(2)}) collective-permute-start(f32[64,512]{1,0:T(8,128)} %shard_map.49), channel_id=1, source_target_pairs={{0,16},{16,32},{32,48},{48,64},{64,80},{80,96},{96,112},{112,128},... | collective-permute-start | bytes 393224 | tf_op jit(solution)/shard_map/ppermute | solution.py:385
  57.1 13.1 %collective-permute-start.2 = (f32[384,128]{1,0:T(8,128)S(1)}, f32[384,128]{1,0:T(8,128)S(1)}, u32[]{:S(2)}, u32[]{:S(2)}) collective-permute-start(f32[384,128]{1,0:T(8,128)S(1)} %bitcast.13), channel_id=1, source_target_pairs={{0,240},{16,0},{32,16},{48,32},{64,48},{80,64},{96,80},{112,96},{1... | collective-permute-start | bytes 589832 | tf_op jit(solution)/shard_map/ppermute | solution.py:385

commit v5 on v4

--- a/solution.py
+++ b/solution.py
@@ -410,7 +410,7 @@
     f32 = jnp.float32
     shape = jax.ShapeDtypeStruct
     x = child_patterns.reshape(parts, boxes * kids * half_rows, cols)
-    work = pltpu.VMEM((boxes * 512, LANES), f32)
+    work = pltpu.VMEM((boxes * 512 + 8, LANES), f32)
     sems = pltpu.SemaphoreType.DMA((parts, boxes))
     edge = len(EDGE_ROWS)
 
@@ -484,7 +484,7 @@
     out = call(
         outer_kernel,
         shape(x.shape, f32),
-        [pltpu.VMEM(x.shape, f32), pltpu.VMEM((boxes * 256, LANES), f32), sems],
+        [pltpu.VMEM(x.shape, f32), pltpu.VMEM((boxes * 256 + 8, LANES), f32), sems],
         10**7,
         2 * 10**6,
         from_next,

time: 72.2 us -> 72.2 us (level)
  no operation moved by 1% of the time
where the time goes in v5:
time: 72.2 us; the launch traced here: 71.9 us
  starting transfers between devices  22.8 us (32%)
  blocking collectives  18 us (25%)
  waiting for transfers between devices  16 us (22%)
  Pallas kernels  13.8 us (19%)
  local copies, waits for them, and re-layouts  1.27 us (2%)
    all_to_all x1, blocking collectives, on_device(): received = lax.all_to_all(received, 'box', 0, 0, tiled=True)  18 us
    pallas_call x8, Pallas kernels, call(): pl.pallas_call(kernel, out_shape=outs, in_specs=[far if i in in_hbm else...  13.8 us
    ppermute x3, starting transfers between devices, to_next(): lax.ppermute(value, 'dir', [(i, (i + step) % size) for i in range(size)])  11.9 us
    all_to_all x1, starting transfers between devices, on_device(): lax.all_to_all(parent.reshape(local_rows, 72, LANES), 'box', 0, 0, tiled=...  10.9 us
    all_to_all x1, waiting for transfers between devices, on_device(): lax.all_to_all(parent.reshape(local_rows, 72, LANES), 'box', 0, 0, tiled=...  8.26 us
    ppermute x3, waiting for transfers between devices, to_next(): lax.ppermute(value, 'dir', [(i, (i + step) % size) for i in range(size)])  7.73 us
  transfers between devices with their start and end apart: 4, of which 4 were waited for; matrix products, arithmetic and copies ran while one was open for 0% of the time, Pallas kernels for 9%

profile of v5, /device:TPU:1, one launch (start us, length us, event | category | flops | bytes accessed | tf_op | source)
XLA Modules:
  0.0 71.9 jit_solution(15281593187638906678)
XLA Ops:
  0.0 0.0 copy-start.1
  0.0 0.0 copy-start
  0.0 1.3 %copy.8 = f32[2,8,8,8,256]{4,3,2,1,0:T(8,128)S(1)} copy(f32[2,8,8,8,256]{4,3,2,1,0:T(8,128)} %param.4) | data formatting | bytes 2097152
  1.3 0.8 %shard_map.46 = (f32[384,128]{1,0:T(8,128)S(1)}, f32[384,128]{1,0:T(8,128)S(1)}, f32[2,512,256]{2,1,0:T(8,128)S(1)}) custom-call(f32[2,512,256]{2,1,0:T(8,128)S(1)} %bitcast.8), custom_call_target="tpu_custom_call", output_to_operand_aliasing={{2}: (0, {})} | custom-call | flops 10000000 | bytes 1000000 | tf_op jit(solution)/shard_map/pallas_call | solution.py:392
  2.1 2.7 %collective-permute-start = (f32[384,128]{1,0:T(8,128)S(1)}, f32[384,128]{1,0:T(8,128)S(1)}, u32[]{:S(2)}, u32[]{:S(2)}) collective-permute-start(f32[384,128]{1,0:T(8,128)S(1)} %get-tuple-element.20), channel_id=1, source_target_pairs={{0,16},{16,32},{32,48},{48,64},{64,80},{80,96},{96,112},{112,128},... | collective-permute-start | bytes 589832 | tf_op jit(solution)/shard_map/ppermute | solution.py:385
  4.8 0.0 copy-done.1
  4.8 0.0 copy-done
  4.8 1.7 %shard_map.47 = (f32[1152,128]{1,0:T(8,128)S(1)}, f32[1024,128]{1,0:T(8,128)S(1)}) custom-call(f32[2,512,256]{2,1,0:T(8,128)S(1)} %get-tuple-element.15.x_ref, s32[16,24]{1,0:T(8,128)S(1)} %pad_add_fusion.lists_ref), custom_call_target="tpu_custom_call" | custom-call | flops 20000000 | bytes 4000000 | tf_op jit(solution)/shard_map/pallas_call | solution.py:392
  6.5 0.9 %collective-permute-done.edge_ref = f32[384,128]{1,0:T(8,128)S(1)} collective-permute-done((f32[384,128]{1,0:T(8,128)S(1)}, f32[384,128]{1,0:T(8,128)S(1)}, u32[]{:S(2)}, u32[]{:S(2)}) %collective-permute-start) | collective-permute-done | bytes 196640 | tf_op jit(solution)/shard_map/ppermute | solution.py:385
  7.4 0.9 %shard_map.48 = f32[1152,128]{1,0:T(8,128)} custom-call(f32[1152,128]{1,0:T(8,128)S(1)} %get-tuple-element.19.own_ref, f32[384,128]{1,0:T(8,128)S(1)} %collective-permute-done.edge_ref), custom_call_target="tpu_custom_call" | custom-call | flops 100000 | bytes 1000000 | tf_op jit(solution)/shard_map/pallas_call | solution.py:392
  8.2 10.9 %all-to-all-start = ((f32[16,72,128]{2,1,0:T(8,128)}), f32[16,72,128]{2,1,0:T(8,128)S(1)}, u32[]{:S(2)}, u32[]{:S(2)}) async-start(f32[16,72,128]{2,1,0:T(8,128)} %bitcast.1), calls=%async_computation | async-start | bytes 1179648 | tf_op jit(solution)/shard_map/all_to_all | solution.py:461
  19.2 2.0 %shard_map.49 = f32[64,512]{1,0:T(8,128)} custom-call(f32[64,16,512]{2,1,0:T(8,128)} %bitcast.12), custom_call_target="tpu_custom_call" | custom-call | flops 20000000 | bytes 4000000 | tf_op jit(solution)/shard_map/pallas_call | solution.py:392
  21.2 2.8 %collective-permute-start.1 = (f32[64,512]{1,0:T(8,128)}, f32[64,512]{1,0:T(8,128)S(1)}, u32[]{:S(2)}, u32[]{:S(2)}) collective-permute-start(f32[64,512]{1,0:T(8,128)} %shard_map.49), channel_id=1, source_target_pairs={{0,16},{16,32},{32,48},{48,64},{64,80},{80,96},{96,112},{112,128},... | collective-permute-start | bytes 393224 | tf_op jit(solution)/shard_map/ppermute | solution.py:385
  24.0 2.3 %collective-permute-done.1 = f32[64,512]{1,0:T(8,128)S(1)} collective-permute-done((f32[64,512]{1,0:T(8,128)}, f32[64,512]{1,0:T(8,128)S(1)}, u32[]{:S(2)}, u32[]{:S(2)}) %collective-permute-start.1) | collective-permute-done | bytes 131104 | tf_op jit(solution)/shard_map/ppermute | solution.py:385
  26.3 0.3 shard_map.50.operator_ref
  26.6 8.3 %all-to-all-done = f32[16,72,128]{2,1,0:T(8,128)S(1)} async-done(((f32[16,72,128]{2,1,0:T(8,128)}), f32[16,72,128]{2,1,0:T(8,128)S(1)}, u32[]{:S(2)}, u32[]{:S(2)}) %all-to-all-start) | async-done | bytes 589856 | tf_op jit(solution)/shard_map/all_to_all | solution.py:461
  34.9 4.2 %shard_map.51 = f32[1024,128]{1,0:T(8,128)S(1)} custom-call(f32[1152,128]{1,0:T(8,128)S(1)} %bitcast.10, f32[528,128]{1,0:T(8,128)S(1)} %shard_map.50.operator_ref), custom_call_target="tpu_custom_call" | custom-call | flops 20000000 | bytes 2000000 | tf_op jit(solution)/shard_map/pallas_call | solution.py:392
  39.1 18.0 %all_to_all.10 = f32[16,64,128]{2,1,0:T(8,128)S(1)} all-to-all(f32[16,64,128]{2,1,0:T(8,128)S(1)} %bitcast.11), channel_id=1, replica_groups=mesh['dir'=16,'box'=16] {'box'}, dimensions={0} | all-to-all | bytes 1048576 | tf_op jit(solution)/shard_map/all_to_all | solution.py:478
  57.1 6.4 %collective-permute-start.2 = (f32[384,128]{1,0:T(8,128)S(1)}, f32[384,128]{1,0:T(8,128)S(1)}, u32[]{:S(2)}, u32[]{:S(2)}) collective-permute-start(f32[384,128]{1,0:T(8,128)S(1)} %bitcast.13), channel_id=1, source_target_pairs={{0,240},{16,0},{32,16},{48,32},{64,48},{80,64},{96,80},{112,96},{1... | collective-permute-start | bytes 589832 | tf_op jit(solution)/shard_map/ppermute | solution.py:385
  63.5 2.2 %shard_map.52.part_ref = f32[2,512,256]{2,1,0:T(8,128)S(1)} custom-call(f32[1024,128]{1,0:T(8,128)S(1)} %bitcast.9, f32[1024,128]{1,0:T(8,128)S(1)} %get-tuple-element.24.table), custom_call_target="tpu_custom_call" | custom-call | flops 20000000 | bytes 4000000 | tf_op jit(solution)/shard_map/pallas_call | solution.py:392
  65.7 4.6 %collective-permute-done.2.edge_ref = f32[384,128]{1,0:T(8,128)S(1)} collective-permute-done((f32[384,128]{1,0:T(8,128)S(1)}, f32[384,128]{1,0:T(8,128)S(1)}, u32[]{:S(2)}, u32[]{:S(2)}) %collective-permute-start.2) | collective-permute-done | bytes 196640 | tf_op jit(solution)/shard_map/ppermute | solution.py:385
  70.2 1.7 %shard_map.53 = f32[2,512,256]{2,1,0:T(8,128)} custom-call(f32[384,128]{1,0:T(8,128)S(1)} %collective-permute-done.2.edge_ref, f32[384,128]{1,0:T(8,128)S(1)} %get-tuple-element.23.table, f32[2,512,256]{2,1,0:T(8,128)S(1)} %shard_map.52.part_ref), custom_call_target="tpu_custom_call" | custom-call | flops 10000000 | bytes 2000000 | tf_op jit(solution)/shard_map/pallas_call | solution.py:392
  (3 shorter events, 0.0 us)
Async XLA Ops:
  0.0 4.8 %copy-start.1 = (s32[8,24]{1,0:T(8,128)S(1)}, s32[8,24]{1,0:T(8,128)}, u32[]{:S(2)}) copy-start(s32[8,24]{1,0:T(8,128)} %param.6) | copy-start | bytes 2308
  0.0 4.8 %copy-start = (s32[8,24]{1,0:T(8,128)S(1)}, s32[8,24]{1,0:T(8,128)}, u32[]{:S(2)}) copy-start(s32[8,24]{1,0:T(8,128)} %param.7) | copy-start | bytes 2308
  2.1 5.3 %collective-permute-start = (f32[384,128]{1,0:T(8,128)S(1)}, f32[384,128]{1,0:T(8,128)S(1)}, u32[]{:S(2)}, u32[]{:S(2)}) collective-permute-start(f32[384,128]{1,0:T(8,128)S(1)} %get-tuple-element.20), channel_id=1, source_target_pairs={{0,16},{16,32},{32,48},{48,64},{64,80},{80,96},{96,112},{112,128},... | collective-permute-start | bytes 589832 | tf_op jit(solution)/shard_map/ppermute | solution.py:385
  8.2 26.6 %all-to-all-start = ((f32[16,72,128]{2,1,0:T(8,128)}), f32[16,72,128]{2,1,0:T(8,128)S(1)}, u32[]{:S(2)}, u32[]{:S(2)}) async-start(f32[16,72,128]{2,1,0:T(8,128)} %bitcast.1), calls=%async_computation | async-start | bytes 1179648 | tf_op jit(solution)/shard_map/all_to_all | solution.py:461
  21.2 5.1 %collective-permute-start.1 = (f32[64,512]{1,0:T(8,128)}, f32[64,512]{1,0:T(8,128)S(1)}, u32[]{:S(2)}, u32[]{:S(2)}) collective-permute-start(f32[64,512]{1,0:T(8,128)} %shard_map.49), channel_id=1, source_target_pairs={{0,16},{16,32},{32,48},{48,64},{64,80},{80,96},{96,112},{112,128},... | collective-permute-start | bytes 393224 | tf_op jit(solution)/shard_map/ppermute | solution.py:385
  57.1 13.1 %collective-permute-start.2 = (f32[384,128]{1,0:T(8,128)S(1)}, f32[384,128]{1,0:T(8,128)S(1)}, u32[]{:S(2)}, u32[]{:S(2)}) collective-permute-start(f32[384,128]{1,0:T(8,128)S(1)} %bitcast.13), channel_id=1, source_target_pairs={{0,240},{16,0},{32,16},{48,32},{64,48},{80,64},{96,80},{112,96},{1... | collective-permute-start | bytes 589832 | tf_op jit(solution)/shard_map/ppermute | solution.py:385

commit v6 on v5

--- a/solution.py
+++ b/solution.py
@@ -94,7 +94,7 @@
 def azimuth_weights(cols, transpose):
     i = lax.broadcasted_iota(jnp.int32, (cols, cols), 0)
     j = lax.broadcasted_iota(jnp.int32, (cols, cols), 1)
-    shift = (j - i if transpose else i - j) % cols
+    shift = (j - i if transpose else i - j) & (cols - 1)
     near = (shift == 0) | (shift == 1)
     far = (shift == cols - 1) | (shift == 2)
     return jnp.where(near, 0.5625, jnp.where(far, -0.0625, 0.0)).astype(jnp.bfloat16)
@@ -349,11 +349,9 @@
     def get_row(i, b):
         return edge_ref[pl.ds(pl.multiple_of(i * 64 + b * 8, 8), 8), :]
 
-    def copy(part, b):
+    def copy(b):
         at = pl.ds(pl.multiple_of(b * 64, 64), 64)
-        return pltpu.make_async_copy(
-            out_ref.at[part, at, :], out_hbm.at[part, at, :], sems.at[part, b]
-        )
+        return pltpu.make_async_copy(out_ref.at[:, at, :], out_hbm.at[:, at, :], sems.at[b])
 
     blank = jnp.zeros((4, cols), jnp.float32)
 
@@ -371,13 +369,12 @@
             for c in range(KIDS):
                 pieces += [blank, values[part][c * 4 : c * 4 + 4]]
             out_ref[part, at, :] = part_ref[part, at, :] + jnp.concatenate(pieces, axis=0)
-            copy(part, b).start()
+        copy(b).start()
         return carry
 
     lax.fori_loop(0, boxes, box, 0, unroll=8)
     for b in range(boxes):
-        for part in range(2):
-            copy(part, b).wait()
+        copy(b).wait()
 
 
 def to_next(value, step):
@@ -411,7 +408,7 @@
     shape = jax.ShapeDtypeStruct
     x = child_patterns.reshape(parts, boxes * kids * half_rows, cols)
     work = pltpu.VMEM((boxes * 512 + 8, LANES), f32)
-    sems = pltpu.SemaphoreType.DMA((parts, boxes))
+    sems = pltpu.SemaphoreType.DMA((boxes,))
     edge = len(EDGE_ROWS)
 
     share, edge_table, x = call(

time: 72.2 us -> 72 us (level)
  transfers between devices with their start and end apart: 4 -> 4, of which waited for: 4 -> 4; matrix products, arithmetic and copies ran while one was open for 0% -> 0% of each run, Pallas kernels for 9% -> 8%
where the time goes in v6:
time: 72 us; the launch traced here: 71.7 us
  starting transfers between devices  22.8 us (32%)
  blocking collectives  18 us (25%)
  waiting for transfers between devices  16.1 us (22%)
  Pallas kernels  13.4 us (19%)
  local copies, waits for them, and re-layouts  1.27 us (2%)
    all_to_all x1, blocking collectives, on_device(): received = lax.all_to_all(received, 'box', 0, 0, tiled=True)  18 us
    pallas_call x8, Pallas kernels, call(): pl.pallas_call(kernel, out_shape=outs, in_specs=[far if i in in_hbm else...  13.4 us
    ppermute x3, starting transfers between devices, to_next(): lax.ppermute(value, 'dir', [(i, (i + step) % size) for i in range(size)])  11.9 us
    all_to_all x1, starting transfers between devices, on_device(): lax.all_to_all(parent.reshape(local_rows, 72, LANES), 'box', 0, 0, tiled=...  10.9 us
    all_to_all x1, waiting for transfers between devices, on_device(): lax.all_to_all(parent.reshape(local_rows, 72, LANES), 'box', 0, 0, tiled=...  8.25 us
    ppermute x3, waiting for transfers between devices, to_next(): lax.ppermute(value, 'dir', [(i, (i + step) % size) for i in range(size)])  7.88 us
  transfers between devices with their start and end apart: 4, of which 4 were waited for; matrix products, arithmetic and copies ran while one was open for 0% of the time, Pallas kernels for 8%

profile of v6, /device:TPU:1, one launch (start us, length us, event | category | flops | bytes accessed | tf_op | source)
XLA Modules:
  0.0 71.7 jit_solution(13556682480926670185)
XLA Ops:
  0.0 0.0 copy-start.1
  0.0 0.0 copy-start
  0.0 1.3 %copy.8 = f32[2,8,8,8,256]{4,3,2,1,0:T(8,128)S(1)} copy(f32[2,8,8,8,256]{4,3,2,1,0:T(8,128)} %param.4) | data formatting | bytes 2097152
  1.3 0.7 %shard_map.46 = (f32[384,128]{1,0:T(8,128)S(1)}, f32[384,128]{1,0:T(8,128)S(1)}, f32[2,512,256]{2,1,0:T(8,128)S(1)}) custom-call(f32[2,512,256]{2,1,0:T(8,128)S(1)} %bitcast.8), custom_call_target="tpu_custom_call", output_to_operand_aliasing={{2}: (0, {})} | custom-call | flops 10000000 | bytes 1000000 | tf_op jit(solution)/shard_map/pallas_call | solution.py:389
  2.0 2.7 %collective-permute-start = (f32[384,128]{1,0:T(8,128)S(1)}, f32[384,128]{1,0:T(8,128)S(1)}, u32[]{:S(2)}, u32[]{:S(2)}) collective-permute-start(f32[384,128]{1,0:T(8,128)S(1)} %get-tuple-element.20), channel_id=1, source_target_pairs={{0,16},{16,32},{32,48},{48,64},{64,80},{80,96},{96,112},{112,128},... | collective-permute-start | bytes 589832 | tf_op jit(solution)/shard_map/ppermute | solution.py:382
  4.7 0.0 copy-done.1
  4.7 0.0 copy-done
  4.7 1.6 %shard_map.47 = (f32[1152,128]{1,0:T(8,128)S(1)}, f32[1024,128]{1,0:T(8,128)S(1)}) custom-call(f32[2,512,256]{2,1,0:T(8,128)S(1)} %get-tuple-element.15.x_ref, s32[16,24]{1,0:T(8,128)S(1)} %pad_add_fusion.lists_ref), custom_call_target="tpu_custom_call" | custom-call | flops 20000000 | bytes 4000000 | tf_op jit(solution)/shard_map/pallas_call | solution.py:389
  6.3 1.0 %collective-permute-done.edge_ref = f32[384,128]{1,0:T(8,128)S(1)} collective-permute-done((f32[384,128]{1,0:T(8,128)S(1)}, f32[384,128]{1,0:T(8,128)S(1)}, u32[]{:S(2)}, u32[]{:S(2)}) %collective-permute-start) | collective-permute-done | bytes 196640 | tf_op jit(solution)/shard_map/ppermute | solution.py:382
  7.3 0.9 %shard_map.48 = f32[1152,128]{1,0:T(8,128)} custom-call(f32[1152,128]{1,0:T(8,128)S(1)} %get-tuple-element.19.own_ref, f32[384,128]{1,0:T(8,128)S(1)} %collective-permute-done.edge_ref), custom_call_target="tpu_custom_call" | custom-call | flops 100000 | bytes 1000000 | tf_op jit(solution)/shard_map/pallas_call | solution.py:389
  8.2 10.9 %all-to-all-start = ((f32[16,72,128]{2,1,0:T(8,128)}), f32[16,72,128]{2,1,0:T(8,128)S(1)}, u32[]{:S(2)}, u32[]{:S(2)}) async-start(f32[16,72,128]{2,1,0:T(8,128)} %bitcast.1), calls=%async_computation | async-start | bytes 1179648 | tf_op jit(solution)/shard_map/all_to_all | solution.py:458
  19.1 2.0 %shard_map.49 = f32[64,512]{1,0:T(8,128)} custom-call(f32[64,16,512]{2,1,0:T(8,128)} %bitcast.12), custom_call_target="tpu_custom_call" | custom-call | flops 20000000 | bytes 4000000 | tf_op jit(solution)/shard_map/pallas_call | solution.py:389
  21.1 2.8 %collective-permute-start.1 = (f32[64,512]{1,0:T(8,128)}, f32[64,512]{1,0:T(8,128)S(1)}, u32[]{:S(2)}, u32[]{:S(2)}) collective-permute-start(f32[64,512]{1,0:T(8,128)} %shard_map.49), channel_id=1, source_target_pairs={{0,16},{16,32},{32,48},{48,64},{64,80},{80,96},{96,112},{112,128},... | collective-permute-start | bytes 393224 | tf_op jit(solution)/shard_map/ppermute | solution.py:382
  23.9 2.3 %collective-permute-done.1 = f32[64,512]{1,0:T(8,128)S(1)} collective-permute-done((f32[64,512]{1,0:T(8,128)}, f32[64,512]{1,0:T(8,128)S(1)}, u32[]{:S(2)}, u32[]{:S(2)}) %collective-permute-start.1) | collective-permute-done | bytes 131104 | tf_op jit(solution)/shard_map/ppermute | solution.py:382
  26.2 0.3 shard_map.50.operator_ref
  26.5 8.3 %all-to-all-done = f32[16,72,128]{2,1,0:T(8,128)S(1)} async-done(((f32[16,72,128]{2,1,0:T(8,128)}), f32[16,72,128]{2,1,0:T(8,128)S(1)}, u32[]{:S(2)}, u32[]{:S(2)}) %all-to-all-start) | async-done | bytes 589856 | tf_op jit(solution)/shard_map/all_to_all | solution.py:458
  34.8 4.2 %shard_map.51 = f32[1024,128]{1,0:T(8,128)S(1)} custom-call(f32[1152,128]{1,0:T(8,128)S(1)} %bitcast.10, f32[528,128]{1,0:T(8,128)S(1)} %shard_map.50.operator_ref), custom_call_target="tpu_custom_call" | custom-call | flops 20000000 | bytes 2000000 | tf_op jit(solution)/shard_map/pallas_call | solution.py:389
  39.0 18.0 %all_to_all.10 = f32[16,64,128]{2,1,0:T(8,128)S(1)} all-to-all(f32[16,64,128]{2,1,0:T(8,128)S(1)} %bitcast.11), channel_id=1, replica_groups=mesh['dir'=16,'box'=16] {'box'}, dimensions={0} | all-to-all | bytes 1048576 | tf_op jit(solution)/shard_map/all_to_all | solution.py:475
  57.0 6.4 %collective-permute-start.2 = (f32[384,128]{1,0:T(8,128)S(1)}, f32[384,128]{1,0:T(8,128)S(1)}, u32[]{:S(2)}, u32[]{:S(2)}) collective-permute-start(f32[384,128]{1,0:T(8,128)S(1)} %bitcast.13), channel_id=1, source_target_pairs={{0,240},{16,0},{32,16},{48,32},{64,48},{80,64},{96,80},{112,96},{1... | collective-permute-start | bytes 589832 | tf_op jit(solution)/shard_map/ppermute | solution.py:382
  63.4 2.1 %shard_map.52.part_ref = f32[2,512,256]{2,1,0:T(8,128)S(1)} custom-call(f32[1024,128]{1,0:T(8,128)S(1)} %bitcast.9, f32[1024,128]{1,0:T(8,128)S(1)} %get-tuple-element.24.table), custom_call_target="tpu_custom_call" | custom-call | flops 20000000 | bytes 4000000 | tf_op jit(solution)/shard_map/pallas_call | solution.py:389
  65.5 4.6 %collective-permute-done.2.edge_ref = f32[384,128]{1,0:T(8,128)S(1)} collective-permute-done((f32[384,128]{1,0:T(8,128)S(1)}, f32[384,128]{1,0:T(8,128)S(1)}, u32[]{:S(2)}, u32[]{:S(2)}) %collective-permute-start.2) | collective-permute-done | bytes 196640 | tf_op jit(solution)/shard_map/ppermute | solution.py:382
  70.2 1.6 %shard_map.53 = f32[2,512,256]{2,1,0:T(8,128)} custom-call(f32[384,128]{1,0:T(8,128)S(1)} %collective-permute-done.2.edge_ref, f32[384,128]{1,0:T(8,128)S(1)} %get-tuple-element.23.table, f32[2,512,256]{2,1,0:T(8,128)S(1)} %shard_map.52.part_ref), custom_call_target="tpu_custom_call" | custom-call | flops 10000000 | bytes 2000000 | tf_op jit(solution)/shard_map/pallas_call | solution.py:389
  (3 shorter events, 0.0 us)
Async XLA Ops:
  0.0 4.7 %copy-start.1 = (s32[8,24]{1,0:T(8,128)S(1)}, s32[8,24]{1,0:T(8,128)}, u32[]{:S(2)}) copy-start(s32[8,24]{1,0:T(8,128)} %param.6) | copy-start | bytes 2308
  0.0 4.7 %copy-start = (s32[8,24]{1,0:T(8,128)S(1)}, s32[8,24]{1,0:T(8,128)}, u32[]{:S(2)}) copy-start(s32[8,24]{1,0:T(8,128)} %param.7) | copy-start | bytes 2308
  2.0 5.3 %collective-permute-start = (f32[384,128]{1,0:T(8,128)S(1)}, f32[384,128]{1,0:T(8,128)S(1)}, u32[]{:S(2)}, u32[]{:S(2)}) collective-permute-start(f32[384,128]{1,0:T(8,128)S(1)} %get-tuple-element.20), channel_id=1, source_target_pairs={{0,16},{16,32},{32,48},{48,64},{64,80},{80,96},{96,112},{112,128},... | collective-permute-start | bytes 589832 | tf_op jit(solution)/shard_map/ppermute | solution.py:382
  8.2 26.6 %all-to-all-start = ((f32[16,72,128]{2,1,0:T(8,128)}), f32[16,72,128]{2,1,0:T(8,128)S(1)}, u32[]{:S(2)}, u32[]{:S(2)}) async-start(f32[16,72,128]{2,1,0:T(8,128)} %bitcast.1), calls=%async_computation | async-start | bytes 1179648 | tf_op jit(solution)/shard_map/all_to_all | solution.py:458
  21.1 5.1 %collective-permute-start.1 = (f32[64,512]{1,0:T(8,128)}, f32[64,512]{1,0:T(8,128)S(1)}, u32[]{:S(2)}, u32[]{:S(2)}) collective-permute-start(f32[64,512]{1,0:T(8,128)} %shard_map.49), channel_id=1, source_target_pairs={{0,16},{16,32},{32,48},{48,64},{64,80},{80,96},{96,112},{112,128},... | collective-permute-start | bytes 393224 | tf_op jit(solution)/shard_map/ppermute | solution.py:382
  57.0 13.1 %collective-permute-start.2 = (f32[384,128]{1,0:T(8,128)S(1)}, f32[384,128]{1,0:T(8,128)S(1)}, u32[]{:S(2)}, u32[]{:S(2)}) collective-permute-start(f32[384,128]{1,0:T(8,128)S(1)} %bitcast.13), channel_id=1, source_target_pairs={{0,240},{16,0},{32,16},{48,32},{64,48},{80,64},{96,80},{112,96},{1... | collective-permute-start | bytes 589832 | tf_op jit(solution)/shard_map/ppermute | solution.py:382
